TPU v7x, 32 devices: a whole 2x2x4 slice. The times are simulated.
32 devices in a mesh: groups: 2 (over y), seq: 4 (over z), tensor: 4 (over x, core).
Axes of the slice: x: 2, y: 2, z: 4, core: 2. Of those that a mesh axis runs over, the one named last changes fastest.
Arguments:
- queries: bfloat16 [2048, 4096], P(('groups', 'seq'), 'tensor'), parts along dimension 0, may hold values from -6 to 6
- key_rows: bfloat16 [2048, 2048], P(('groups', 'seq'), 'tensor'), parts along dimension 0, may hold values from -6 to 6
- value_rows: bfloat16 [2048, 2048], P(('groups', 'seq'), 'tensor'), parts along dimension 0, may hold values from -6 to 6
- positions: int32 [2048], P(('groups', 'seq')), parts along dimension 0, may hold values from 0 to 131071, as said below
- residual: bfloat16 [2048, 3840], P(('groups', 'seq'), 'tensor'), parts along dimension 0, may hold values from -16 to 16
- direction: float32 [7680], P('groups'), parts along dimension 0, may hold values from -90 to 90
- out_weight: bfloat16 [4096, 3840], P('tensor'), may hold values from -0.375 to 0.375
Outputs:
- ablated: bfloat16 [2048, 3840], P(('groups', 'seq'), 'tensor'), parts along dimension 0
There are 2 independent parts, one for each index of `groups`. A program takes and returns all parts, laid end to end along the dimension named above; an argument that names none is the same for every part. Nothing has to cross between parts.
Inputs may be any that keep to these rules, and one draw needn't show every extreme that they name: positions strictly increase along the slab, by at most 4 from one token to the next; the slab ends at the prompt's last position.
All inputs are finite; a program needn't handle non-finite values.
Results may differ from a plain program's by a relative error of at most 0.017.
Values may be sent and summed in bfloat16 or wider, within the bound.
A program may use at most 64 MiB of HBM per device.

v0:
```python
import jax
import jax.numpy as jnp
from jax import lax
from jax.sharding import PartitionSpec as P

HD = 256
WINDOW = 1024


big_negative = -1e30


def shifted_2(value, axis, steps):
    count = lax.axis_size(axis)
    first, last = (max(0, -steps), min(count, count - steps))
    return lax.ppermute(value, axis, [(source, source + steps) for source in range(first, last)])


def rotary_tables(positions, head_dim):
    half_dim = head_dim // 2
    freqs = jnp.power(10000.0, -jnp.arange(half_dim, dtype=jnp.float32) * 2.0 / head_dim)
    angles = positions.astype(jnp.float32)[:, None] * freqs[None, :]
    return (jnp.cos(angles)[:, None, :], jnp.sin(angles)[:, None, :])


def rotate_heads(block, cos_table, sin_table, head_dim):
    row_count = block.shape[0]
    head_count = block.shape[1] // head_dim
    half_dim = head_dim // 2
    widened = block.reshape(row_count, head_count, head_dim).astype(jnp.float32)
    first_half = widened[:, :, :half_dim]
    second_half = widened[:, :, half_dim:]
    turned = jnp.concatenate(
        [
            first_half * cos_table - second_half * sin_table,
            second_half * cos_table + first_half * sin_table,
        ],
        axis=-1,
    )
    return turned.reshape(row_count, head_count * head_dim)


def body(queries, key_rows, value_rows, positions, residual, direction, out_weight):
    tokens_here = queries.shape[0]
    query_heads = queries.shape[1] // HD
    kv_heads = key_rows.shape[1] // HD
    group_size = query_heads // kv_heads
    span_blocks = WINDOW // tokens_here
    seq_index = lax.axis_index("seq")
    cos_table, sin_table = rotary_tables(positions, HD)
    rot_queries = (rotate_heads(queries, cos_table, sin_table, HD) * HD ** (-0.5)).astype(
        jnp.bfloat16
    )
    rot_keys = rotate_heads(key_rows, cos_table, sin_table, HD).astype(jnp.bfloat16)
    query_blocks = rot_queries.reshape(tokens_here, kv_heads, group_size, HD)
    own_scores = jnp.einsum(
        "qkgd,skd->kgqs",
        query_blocks,
        rot_keys.reshape(tokens_here, kv_heads, HD),
        preferred_element_type=jnp.float32,
    )
    earlier_keys = []
    earlier_values = []
    for distance in range(span_blocks, 0, -1):
        moved_keys, moved_values = shifted_2((rot_keys, value_rows), "seq", distance)
        earlier_keys.append(moved_keys)
        earlier_values.append(moved_values)
    far_keys = jnp.concatenate(earlier_keys, axis=0)
    far_values = jnp.concatenate(earlier_values, axis=0)
    far_scores = jnp.einsum(
        "qkgd,skd->kgqs",
        query_blocks,
        far_keys.reshape(-1, kv_heads, HD),
        preferred_element_type=jnp.float32,
    )
    scores = jnp.concatenate([far_scores, own_scores], axis=-1)
    query_index = seq_index * tokens_here + jnp.arange(tokens_here, dtype=jnp.int32)
    key_index = (seq_index - span_blocks) * tokens_here + jnp.arange(
        (span_blocks + 1) * tokens_here, dtype=jnp.int32
    )
    gap_grid = query_index[:, None] - key_index[None, :]
    allowed = (gap_grid >= 0) & (gap_grid < WINDOW) & (key_index[None, :] >= 0)
    scores = jnp.where(allowed, scores, big_negative)
    row_max = jnp.max(scores, axis=-1, keepdims=True)
    shifted = jnp.exp(scores - row_max)
    row_sum = jnp.sum(shifted, axis=-1, keepdims=True)
    weights = (shifted / row_sum).astype(jnp.bfloat16)
    every_value = jnp.concatenate([far_values, value_rows], axis=0).reshape(-1, kv_heads, HD)
    mixed = jnp.einsum("kgqs,skd->qkgd", weights, every_value, preferred_element_type=jnp.float32)
    attended = mixed.astype(jnp.bfloat16).reshape(tokens_here, query_heads * HD)
    partial_value = jnp.dot(attended, out_weight, preferred_element_type=jnp.float32)
    unit_dir = direction / jnp.sqrt(jnp.sum(direction * direction) + 1e-06)
    column_width = residual.shape[1]
    tensor_index = lax.axis_index("tensor")
    local_dir = lax.dynamic_slice_in_dim(unit_dir, tensor_index * column_width, column_width, 0)
    base_state = residual.astype(jnp.float32)
    rounded_terms = partial_value.astype(jnp.bfloat16).astype(jnp.float32)
    dot_terms = jnp.sum(rounded_terms * unit_dir[None, :], axis=1) + jnp.sum(
        base_state * local_dir[None, :], axis=1
    )
    along = lax.psum(dot_terms, "tensor")
    summed = lax.psum_scatter(
        partial_value.astype(jnp.bfloat16), "tensor", scatter_dimension=1, tiled=True
    ).astype(jnp.float32)
    hidden_state = base_state + summed
    ablated = (hidden_state - along[:, None] * local_dir[None, :]).astype(jnp.bfloat16)
    return ablated


def solution(mesh):
    return jax.shard_map(
        body,
        mesh=mesh,
        in_specs=(
            P(("groups", "seq"), "tensor"),
            P(("groups", "seq"), "tensor"),
            P(("groups", "seq"), "tensor"),
            P(("groups", "seq")),
            P(("groups", "seq"), "tensor"),
            P("groups"),
            P("tensor", None),
        ),
        out_specs=P(("groups", "seq"), "tensor"),
        check_vma=False,
    )
```

profile of v0, /device:TPU:25, one launch (start us, length us, event | category | flops | bytes accessed | tf_op | source)
XLA Modules:
  0.0 116.8 jit_solution(2316174666957197548)
XLA Ops:
  6.5 0.8 collective-permute-start
  7.3 1.3 %collective-permute-start.1 = (bf16[256,512]{1,0:T(8,128)(2,1)}, bf16[256,512]{1,0:T(8,128)(2,1)S(1)}, u32[]{:S(2)}, u32[]{:S(2)}) collective-permute-start(bf16[256,512]{1,0:T(8,128)(2,1)} %param.9), channel_id=1, source_target_pairs={{0,12},{1,13},{2,14},{3,15},{16,28},{17,29},{18,30},{19,31}} | collective-permute-start | bytes 786440 | tf_op jit(solution)/shard_map/ppermute | solution.py:16
  8.6 1.3 %collective-permute-start.2 = (bf16[256,512]{1,0:T(8,128)(2,1)}, bf16[256,512]{1,0:T(8,128)(2,1)S(1)}, u32[]{:S(2)}, u32[]{:S(2)}) collective-permute-start(bf16[256,512]{1,0:T(8,128)(2,1)} %param.9), channel_id=1, source_target_pairs={{0,8},{4,12},{1,9},{5,13},{2,10},{6,14},{3,11},{7,15},{16,24},{20,... | collective-permute-start | bytes 786440 | tf_op jit(solution)/shard_map/ppermute | solution.py:16
  9.9 1.3 %collective-permute-start.3 = (bf16[256,512]{1,0:T(8,128)(2,1)}, bf16[256,512]{1,0:T(8,128)(2,1)S(1)}, u32[]{:S(2)}, u32[]{:S(2)}) collective-permute-start(bf16[256,512]{1,0:T(8,128)(2,1)} %param.9), channel_id=1, source_target_pairs={{0,4},{4,8},{8,12},{1,5},{5,9},{9,13},{2,6},{6,10},{10,14},{3,7},{... | collective-permute-start | bytes 786440 | tf_op jit(solution)/shard_map/ppermute | solution.py:16
  11.3 0.7 convert_element_type.57
  11.9 1.1 copy.37
  13.3 0.5 multiply_cosine_fusion
  14.0 0.8 copy.40
  14.8 1.3 %collective-permute-start.7 = (bf16[256,512]{0,1:T(8,128)(2,1)}, bf16[256,512]{0,1:T(8,128)(2,1)}, u32[]{:S(2)}, u32[]{:S(2)}) collective-permute-start(bf16[256,512]{0,1:T(8,128)(2,1)} %bitcast.5), channel_id=1, source_target_pairs={{0,4},{4,8},{8,12},{1,5},{5,9},{9,13},{2,6},{6,10},{10,14},{3,7},{... | collective-permute-start | bytes 786440 | tf_op jit(solution)/shard_map/ppermute | solution.py:16
  16.2 0.5 reshape.96
  17.0 1.3 %convolution_bitcast_fusion.1 = f32[2,2,256,256]{2,3,1,0:T(8,128)} fusion(bf16[256,2,2,256]{3,0,2,1:T(8,128)(2,1)S(1)} %bitcast.36, bf16[256,2,128]{2,0,1:T(8,128)(2,1)S(1)} %get-tuple-element.10, bf16[256,2,128]{2,0,1:T(8,128)(2,1)S(1)} %get-tuple-element.9), kind=kOutput, calls=%fused_computation.14 | convolution fusion | flops 134742016 | bytes 1835008 | tf_op jit(solution)/shard_map/qkgd,skd->kgqs/dot_general | solution.py:56
  18.4 0.9 fusion.7
  19.3 0.6 multiply_reduce_fusion.1
  20.6 1.3 %collective-permute-start.6 = (bf16[256,512]{0,1:T(8,128)(2,1)}, bf16[256,512]{0,1:T(8,128)(2,1)}, u32[]{:S(2)}, u32[]{:S(2)}) collective-permute-start(bf16[256,512]{0,1:T(8,128)(2,1)} %bitcast.5), channel_id=1, source_target_pairs={{0,8},{4,12},{1,9},{5,13},{2,10},{6,14},{3,11},{7,15},{16,24},{20,... | collective-permute-start | bytes 786440 | tf_op jit(solution)/shard_map/ppermute | solution.py:16
  22.0 1.3 %collective-permute-start.5 = (bf16[256,512]{0,1:T(8,128)(2,1)}, bf16[256,512]{0,1:T(8,128)(2,1)}, u32[]{:S(2)}, u32[]{:S(2)}) collective-permute-start(bf16[256,512]{0,1:T(8,128)(2,1)} %bitcast.5), channel_id=1, source_target_pairs={{0,12},{1,13},{2,14},{3,15},{16,28},{17,29},{18,30},{19,31}} | collective-permute-start | bytes 786440 | tf_op jit(solution)/shard_map/ppermute | solution.py:16
  23.3 7.5 %collective-permute-done.2 = bf16[256,512]{1,0:T(8,128)(2,1)S(1)} collective-permute-done((bf16[256,512]{1,0:T(8,128)(2,1)}, bf16[256,512]{1,0:T(8,128)(2,1)S(1)}, u32[]{:S(2)}, u32[]{:S(2)}) %collective-permute-start.2) | collective-permute-done | bytes 262176 | tf_op jit(solution)/shard_map/ppermute | solution.py:16
  30.8 1.4 %collective-permute-start.4 = (bf16[256,512]{0,1:T(8,128)(2,1)}, bf16[256,512]{0,1:T(8,128)(2,1)}, u32[]{:S(2)}, u32[]{:S(2)}) collective-permute-start(bf16[256,512]{0,1:T(8,128)(2,1)} %bitcast.5), channel_id=1, source_target_pairs={} | collective-permute-start | bytes 786440 | tf_op jit(solution)/shard_map/ppermute | solution.py:16
  32.2 0.6 copy.36
  32.9 3.6 %collective-permute-done.7 = bf16[256,512]{0,1:T(8,128)(2,1)} collective-permute-done((bf16[256,512]{0,1:T(8,128)(2,1)}, bf16[256,512]{0,1:T(8,128)(2,1)}, u32[]{:S(2)}, u32[]{:S(2)}) %collective-permute-start.7) | collective-permute-done | bytes 262176 | tf_op jit(solution)/shard_map/ppermute | solution.py:16
  36.4 22.6 %collective-permute-done.6 = bf16[256,512]{0,1:T(8,128)(2,1)} collective-permute-done((bf16[256,512]{0,1:T(8,128)(2,1)}, bf16[256,512]{0,1:T(8,128)(2,1)}, u32[]{:S(2)}, u32[]{:S(2)}) %collective-permute-start.6) | collective-permute-done | bytes 262176 | tf_op jit(solution)/shard_map/ppermute | solution.py:16
  59.0 1.3 %pad_maximum_fusion = bf16[1024,512]{0,1:T(8,128)(2,1)S(1)} fusion(bf16[256,512]{0,1:T(8,128)(2,1)} %collective-permute-done.7, bf16[256,512]{0,1:T(8,128)(2,1)} %collective-permute-done.6, bf16[256,512]{0,1:T(8,128)(2,1)} %collective-permute-done.5, bf16[256,512]{0,1:T(8,128)(2,1)} %collective-permute-done.4), kind=kLoop, calls=%fused_computation.20 | loop fusion | flops 4194304 | bytes 2097152 | tf_op jit(solution)/shard_map/concatenate | solution.py:68
  60.3 0.9 convolution_bitcast_fusion
  61.3 0.3 copy-done.2
  61.6 1.6 %exponential_reduce_fusion = f32[2,2,256]{2,1,0:T(2,128)S(1)} fusion(f32[2,2,256,256]{2,3,1,0:T(8,128)S(1)} %copy-done.2, f32[2,2,256,1024]{2,3,1,0:T(8,128)S(1)} %convolution_bitcast_fusion, pred[256,1280]{0,1:T(8,128)(4,1)S(1)} %fusion.7), kind=kOutput, calls=%fused_computation.5 | output fusion | flops 5244159 | bytes 5574656 | tf_op jit(solution)/shard_map/sub | solution.py:85
  63.2 0.3 copy-done
  63.5 4.8 %fusion.8 = bf16[2,256,2,256]{3,1,2,0:T(8,128)(2,1)} fusion(bf16[1280,2,256,1]{0,2,3,1:T(8,128)(2,1)S(1)} %bitcast.40, f32[2,2,256]{2,1,0:T(2,128)S(1)} %exponential_reduce_fusion, f32[2,2,256,256]{2,3,1,0:T(8,128)S(1)} %copy-done.3, f32[2,2,256,1024]{2,3,1,0:T(8,128)} %copy-done, pred[256,1280]{0,1:T(8,128)(4,1)S(1)} %fusion.7), kind=kOutput, calls=%fused_computation.17 | convolution fusion | flops 677906688 | bytes 7409664 | tf_op jit(solution)/shard_map/kgqs,skd->qkgd/dot_general | solution.py:89
  68.3 5.7 %multiply_reduce_fusion = (f32[256]{0:T(256)S(1)}, bf16[256,3840]{1,0:T(8,128)(2,1)S(1)}) fusion(f32[3840]{0:T(1024)S(1)} %broadcast_divide_fusion, bf16[256,1024]{0,1:T(8,128)(2,1)} %bitcast.41, bf16[1024,3840]{1,0:T(8,128)(2,1)} %param.13), kind=kOutput, calls=%fused_computation.7 | convolution fusion | flops 2017197824 | bytes 10371072 | tf_op jit(solution)/shard_map/dot_general | solution.py:91
  74.1 2.3 %copy.52 = bf16[256,3840]{0,1:T(8,128)(2,1)} copy(bf16[256,3840]{1,0:T(8,128)(2,1)S(1)} %get-tuple-element.16) | data formatting | bytes 3932160
  76.5 0.2 fusion.12
  76.7 5.5 %psum.7 = f32[256]{0:T(256)S(1)} all-reduce(f32[256]{0:T(256)S(1)} %add.55), channel_id=1, replica_groups=mesh['groups'=2,'seq'=4,'tensor'=4] {'tensor'}, use_global_device_ids=true, to_apply=%region_6.7 | all-reduce | flops 256 | bytes 2048 | tf_op jit(solution)/shard_map/psum | solution.py:101
  82.2 25.7 %reduce-scatter.4.cloned.1.call-done = bf16[960,256]{1,0:T(8,128)(2,1)} async-done(((bf16[3840,256]{1,0:T(8,128)(2,1)}), bf16[960,256]{1,0:T(8,128)(2,1)}) %reduce-scatter.4.cloned.1.call-update) | async-done | bytes 491536
  108.0 2.0 %fusion.11 = bf16[256,960]{0,1:T(8,128)(2,1)} fusion(bf16[256,960]{0,1:T(8,128)(2,1)S(1)} %copy-done.1, bf16[960,256]{1,0:T(8,128)(2,1)} %reduce-scatter.4.cloned.1.call-done, f32[256]{0:T(256)S(1)} %psum.7, f32[960]{0:T(1024)S(1)} %dynamic_slice.3), kind=kLoop, calls=%fused_computation.24 | loop fusion | flops 1474560 | bytes 1479424 | tf_op jit(solution)/shard_map/convert_element_type | solution.py:106
  (39 shorter events, 1.1 us)
Async XLA Ops:
  6.5 9.6 %copy-start.4 = (bf16[256,1024]{1,0:T(8,128)(2,1)S(1)}, bf16[256,1024]{1,0:T(8,128)(2,1)}, u32[]{:S(2)}) copy-start(bf16[256,1024]{1,0:T(8,128)(2,1)} %param.7) | copy-start | bytes 1572868
  6.5 101.4 %reduce-scatter.4.cloned.1.call-start = ((), (), s32[]{:S(2)}) async-start(), calls=%async_computation.1 | async-start | bytes 2457600
  6.5 14.1 %collective-permute-start = (bf16[256,512]{1,0:T(8,128)(2,1)}, bf16[256,512]{1,0:T(8,128)(2,1)S(1)}, u32[]{:S(2)}, u32[]{:S(2)}) collective-permute-start(bf16[256,512]{1,0:T(8,128)(2,1)} %param.9), channel_id=1, source_target_pairs={} | collective-permute-start | bytes 786440 | tf_op jit(solution)/shard_map/ppermute | solution.py:16
  7.3 14.6 %collective-permute-start.1 = (bf16[256,512]{1,0:T(8,128)(2,1)}, bf16[256,512]{1,0:T(8,128)(2,1)S(1)}, u32[]{:S(2)}, u32[]{:S(2)}) collective-permute-start(bf16[256,512]{1,0:T(8,128)(2,1)} %param.9), channel_id=1, source_target_pairs={{0,12},{1,13},{2,14},{3,15},{16,28},{17,29},{18,30},{19,31}} | collective-permute-start | bytes 786440 | tf_op jit(solution)/shard_map/ppermute | solution.py:16
  8.6 22.2 %collective-permute-start.2 = (bf16[256,512]{1,0:T(8,128)(2,1)}, bf16[256,512]{1,0:T(8,128)(2,1)S(1)}, u32[]{:S(2)}, u32[]{:S(2)}) collective-permute-start(bf16[256,512]{1,0:T(8,128)(2,1)} %param.9), channel_id=1, source_target_pairs={{0,8},{4,12},{1,9},{5,13},{2,10},{6,14},{3,11},{7,15},{16,24},{20,... | collective-permute-start | bytes 786440 | tf_op jit(solution)/shard_map/ppermute | solution.py:16
  9.9 22.2 %collective-permute-start.3 = (bf16[256,512]{1,0:T(8,128)(2,1)}, bf16[256,512]{1,0:T(8,128)(2,1)S(1)}, u32[]{:S(2)}, u32[]{:S(2)}) collective-permute-start(bf16[256,512]{1,0:T(8,128)(2,1)} %param.9), channel_id=1, source_target_pairs={{0,4},{4,8},{8,12},{1,5},{5,9},{9,13},{2,6},{6,10},{10,14},{3,7},{... | collective-permute-start | bytes 786440 | tf_op jit(solution)/shard_map/ppermute | solution.py:16
  14.8 21.6 %collective-permute-start.7 = (bf16[256,512]{0,1:T(8,128)(2,1)}, bf16[256,512]{0,1:T(8,128)(2,1)}, u32[]{:S(2)}, u32[]{:S(2)}) collective-permute-start(bf16[256,512]{0,1:T(8,128)(2,1)} %bitcast.5), channel_id=1, source_target_pairs={{0,4},{4,8},{8,12},{1,5},{5,9},{9,13},{2,6},{6,10},{10,14},{3,7},{... | collective-permute-start | bytes 786440 | tf_op jit(solution)/shard_map/ppermute | solution.py:16
  16.8 2.5 %copy-start.6 = (f32[3840]{0:T(1024)S(1)}, f32[3840]{0:T(1024)}, u32[]{:S(2)}) copy-start(f32[3840]{0:T(1024)} %param.12) | copy-start | bytes 46084
  17.0 15.2 %copy-start.5 = (bf16[256,512]{1,0:T(8,128)(2,1)S(1)}, bf16[256,512]{1,0:T(8,128)(2,1)}, u32[]{:S(2)}) copy-start(bf16[256,512]{1,0:T(8,128)(2,1)} %param.9) | copy-start | bytes 786436
  20.6 38.3 %collective-permute-start.6 = (bf16[256,512]{0,1:T(8,128)(2,1)}, bf16[256,512]{0,1:T(8,128)(2,1)}, u32[]{:S(2)}, u32[]{:S(2)}) collective-permute-start(bf16[256,512]{0,1:T(8,128)(2,1)} %bitcast.5), channel_id=1, source_target_pairs={{0,8},{4,12},{1,9},{5,13},{2,10},{6,14},{3,11},{7,15},{16,24},{20,... | collective-permute-start | bytes 786440 | tf_op jit(solution)/shard_map/ppermute | solution.py:16
  22.0 37.0 %collective-permute-start.5 = (bf16[256,512]{0,1:T(8,128)(2,1)}, bf16[256,512]{0,1:T(8,128)(2,1)}, u32[]{:S(2)}, u32[]{:S(2)}) collective-permute-start(bf16[256,512]{0,1:T(8,128)(2,1)} %bitcast.5), channel_id=1, source_target_pairs={{0,12},{1,13},{2,14},{3,15},{16,28},{17,29},{18,30},{19,31}} | collective-permute-start | bytes 786440 | tf_op jit(solution)/shard_map/ppermute | solution.py:16
  30.8 28.2 %collective-permute-start.4 = (bf16[256,512]{0,1:T(8,128)(2,1)}, bf16[256,512]{0,1:T(8,128)(2,1)}, u32[]{:S(2)}, u32[]{:S(2)}) collective-permute-start(bf16[256,512]{0,1:T(8,128)(2,1)} %bitcast.5), channel_id=1, source_target_pairs={} | collective-permute-start | bytes 786440 | tf_op jit(solution)/shard_map/ppermute | solution.py:16
  60.3 1.2 %copy-start.2 = (f32[2,2,256,256]{2,3,1,0:T(8,128)S(1)}, f32[2,2,256,256]{2,3,1,0:T(8,128)}, u32[]{:S(2)}) copy-start(f32[2,2,256,256]{2,3,1,0:T(8,128)} %convolution_bitcast_fusion.1) | copy-start | bytes 3145732
  61.6 1.9 %copy-start = (f32[2,2,256,1024]{2,3,1,0:T(8,128)}, f32[2,2,256,1024]{2,3,1,0:T(8,128)S(1)}, u32[]{:S(2)}) copy-start(f32[2,2,256,1024]{2,3,1,0:T(8,128)S(1)} %convolution_bitcast_fusion) | copy-start | bytes 12582916
  61.6 2.0 %copy-start.3 = (f32[2,2,256,256]{2,3,1,0:T(8,128)S(1)}, f32[2,2,256,256]{2,3,1,0:T(8,128)}, u32[]{:S(2)}) copy-start(f32[2,2,256,256]{2,3,1,0:T(8,128)} %convolution_bitcast_fusion.1) | copy-start | bytes 3145732
  74.1 2.4 %copy-start.1 = (bf16[256,960]{0,1:T(8,128)(2,1)S(1)}, bf16[256,960]{0,1:T(8,128)(2,1)}, u32[]{:S(2)}) copy-start(bf16[256,960]{0,1:T(8,128)(2,1)} %param.11) | copy-start | bytes 1474564
Sparse Core Ops, SparseCore 0:
  76.5 31.3 reduce-scatter.3
where the time goes:
time: 119 us; the launch traced here: 117 us
  waiting for transfers between devices  59.4 us (50%)
  between operations  14.4 us (12%)
  matrix products  12.8 us (11%)
  starting transfers between devices  9.89 us (8%)
  other arithmetic  8.23 us (7%)
  local copies, waits for them, and re-layouts  6.64 us (6%)
  blocking collectives  5.51 us (5%)
    ppermute x8, waiting for transfers between devices, shifted_2(): lax.ppermute(value, axis, [(source, source + steps) for source in range(f...  33.6 us
    unnamed x2, waiting for transfers between devices  25.8 us
    ppermute x8, starting transfers between devices, shifted_2(): lax.ppermute(value, axis, [(source, source + steps) for source in range(f...  9.89 us
    dot_general x1, matrix products, body(): jnp.dot(attended, out_weight, preferred_element_type=jnp.float32)  5.74 us
    psum x1, blocking collectives, body(): along = lax.psum(dot_terms, 'tensor')  5.51 us
    dot_general x1, matrix products, body(): jnp.einsum('kgqs,skd->qkgd', weights, every_value, preferred_element_type...  4.79 us
    unnamed x22, local copies, waits for them, and re-layouts  4.4 us
  transfers between devices with their start and end apart: 9, of which 4 were waited for; matrix products, arithmetic and copies ran while one was open for 7% of the time, Pallas kernels for 0%

commit v1 on v0

--- a/solution.py
+++ b/solution.py
@@ -1,6 +1,10 @@
+import functools
+
 import jax
 import jax.numpy as jnp
 from jax import lax
+from jax.experimental import pallas as pl
+from jax.experimental.pallas import tpu as pltpu
 from jax.sharding import PartitionSpec as P
 
 HD = 256
@@ -107,9 +111,385 @@
     return ablated
 
 
+BF = jnp.bfloat16
+F32 = jnp.float32
+MESH = pl.DeviceIdType.MESH
+
+(K0A_2, V0A_2, K0B_1, V0B_1, K0A_1, V0A_1, K1A_2, V1A_2, Q3A_2, Q3B_2, Q3B_1, Q2B_1,
+ O3A, L3A, O3B, L3B, OB_0, OB_1, LB_0, LB_1, OC_0, OC_1, LC_0, LC_1, SEQ_COPIES) = range(25)
+
+
+def rot(x, cos, sin):
+    x = x.astype(F32)
+    a, b = x[:, :128], x[:, 128:]
+    return jnp.concatenate([a * cos - b * sin, b * cos + a * sin], axis=1)
+
+
+def attend(q, blocks, diag):
+    scores = [
+        lax.dot_general(k, q, (((1,), (1,)), ((), ())), preferred_element_type=F32)
+        for k, _ in blocks
+    ]
+    if diag:
+        s = scores[-1]
+        key = lax.broadcasted_iota(jnp.int32, s.shape, 0)
+        lane = lax.broadcasted_iota(jnp.int32, s.shape, 1)
+        row = (lane // 256) * 128 + lane % 128
+        scores[-1] = jnp.where(key <= row, s, big_negative)
+    m = functools.reduce(jnp.maximum, [jnp.max(s, axis=0, keepdims=True) for s in scores])
+    acc, l = 0.0, 0.0
+    for s, (_, v) in zip(scores, blocks):
+        p = jnp.exp(s - m)
+        l = l + jnp.sum(p, axis=0, keepdims=True)
+        acc = acc + lax.dot_general(
+            v, p.astype(BF), (((0,), (0,)), ((), ())), preferred_element_type=F32
+        )
+    return acc, m, l
+
+
+def merge(state, out, lse):
+    acc, m, l = state
+    top = jnp.maximum(m, lse)
+    mine, other = jnp.exp(m - top), jnp.exp(lse - top)
+    return acc * mine + out.astype(F32) * other, top, l * mine + other
+
+
+def kernel(q_ref, k_ref, v_ref, cos_ref, sin_ref, res_ref, dir_ref, w_hbm, out_ref,
+           wbuf, rq, rk, kv0, kv1, rq3, rq2, o_a, o_b2, o_b1, l_a, l_b2, l_b1,
+           s_a, s_b2, s_c, t_a, t_b2, t_c, st_acc, st_ml, att, keep,
+           a_send, a_recv, b_send, b_recv, al_send, al_recv,
+           ssem, rsem, wsem, xs, xr, als, alr):
+    s = lax.axis_index("seq")
+    t = lax.axis_index("tensor")
+    core = t % 2
+    x_here = t // 2
+    x_other = 1 - x_here
+    core_peer = t + 1 - 2 * core
+    x_peer = (t + 2) % 4
+    half = wbuf.shape[2]
+    width = half // 2
+
+    def w_copy(i, x):
+        cols = pl.ds(pl.multiple_of(x * half, 128), half)
+        return pltpu.make_async_copy(w_hbm.at[:, cols], wbuf.at[i], wsem.at[i])
+
+    w_copies = [w_copy(0, x_other), w_copy(1, x_here)]
+    for c in w_copies:
+        c.start()
+
+    barrier = pltpu.get_barrier_semaphore()
+    for j in (1, 2, 3):
+        pl.semaphore_signal(barrier, inc=1, device_id={"seq": (s + j) % 4}, device_id_type=MESH)
+        pl.semaphore_signal(barrier, inc=1, device_id={"tensor": (t + j) % 4}, device_id_type=MESH)
+    pl.semaphore_wait(barrier, 6)
+
+    def to(dev, src, dst, si, ri=None):
+        ri = si if ri is None else ri
+        return pltpu.make_async_remote_copy(
+            src_ref=src, dst_ref=dst, send_sem=ssem.at[si], recv_sem=rsem.at[ri],
+            device_id={"seq": dev}, device_id_type=MESH)
+
+    def vcol(g):
+        return v_ref.at[:, 256 * g:256 * g + 256]
+
+    copies = {
+        V0A_2: to(2, vcol(0), kv0.at[1], V0A_2),
+        K0A_2: to(2, rk.at[0], kv0.at[0], K0A_2),
+        V0B_1: to(1, vcol(1), kv0.at[3], V0B_1),
+        K0B_1: to(1, rk.at[1], kv0.at[2], K0B_1),
+        V0A_1: to(1, vcol(0), kv0.at[1], V0A_1),
+        K0A_1: to(1, rk.at[0], kv0.at[0], K0A_1),
+        V1A_2: to(2, vcol(0), kv1.at[1], V1A_2),
+        K1A_2: to(2, rk.at[0], kv1.at[0], K1A_2),
+        Q3A_2: to(2, rq.at[0], rq3.at[0], Q3A_2),
+        Q3B_2: to(2, rq.at[1], rq3.at[1], Q3B_2),
+        Q3B_1: to(1, rq.at[1], rq3.at[1], Q3B_1),
+        Q2B_1: to(1, rq.at[1], rq2, Q2B_1),
+        O3A: to(3, s_a, o_a, O3A),
+        L3A: to(3, t_a, l_a, L3A),
+        O3B: to(3, s_b2, o_b2, O3B),
+        L3B: to(3, t_b2, l_b2, L3B),
+    }
+    for c in (0, 1):
+        copies[OB_0 + c] = to(2, s_c.at[0, c], o_b1.at[c], OB_0 + c)
+        copies[LB_0 + c] = to(2, t_c.at[0, c], l_b1.at[c], LB_0 + c)
+        copies[OC_0 + c] = to(3, s_c.at[1, c], o_b1.at[c], OC_0 + c, OB_0 + c)
+        copies[LC_0 + c] = to(3, t_c.at[1, c], l_b1.at[c], LC_0 + c, LB_0 + c)
+
+    def start(*names):
+        for n in names:
+            copies[n].start()
+
+    def recv(*names):
+        for n in names:
+            copies[n].wait_recv()
+
+    def sent(*names):
+        for n in names:
+            copies[n].wait_send()
+
+    @pl.when(s == 0)
+    def _():
+        start(V0A_2)
+
+    @pl.when(s == 1)
+    def _():
+        start(V1A_2)
+
+    cos, sin = cos_ref[...], sin_ref[...]
+    for g in (0, 1):
+        rk[g] = rot(k_ref[:, 256 * g:256 * g + 256], cos, sin).astype(BF)
+
+    @pl.when(s == 0)
+    def _():
+        start(K0A_2, V0B_1, K0B_1, V0A_1, K0A_1)
+
+    @pl.when(s == 1)
+    def _():
+        start(K1A_2)
+
+    for g in (1, 0):
+        for h in (0, 1):
+            at = 256 * (2 * g + h)
+            r = (rot(q_ref[:, at:at + 256], cos, sin) * HD ** (-0.5)).astype(BF)
+            for c in (0, 1):
+                rq[g, 256 * c + 128 * h:256 * c + 128 * h + 128, :] = r[128 * c:128 * c + 128]
+
+    @pl.when(s == 3)
+    def _():
+        start(Q3B_1, Q3A_2, Q3B_2)
+
+    @pl.when(s == 2)
+    def _():
+        start(Q2B_1)
+
+    def own(g):
+        return rk[g], v_ref[:, 256 * g:256 * g + 256]
+
+    def first(g):
+        return kv0[2 * g], kv0[2 * g + 1]
+
+    def second():
+        return kv1[0], kv1[1]
+
+    def put(g, state, chunks):
+        acc, _, l = state
+        out = acc / l
+        for i, c in enumerate(chunks):
+            for h in (0, 1):
+                at = 256 * i + 128 * h
+                col = 256 * (2 * g + h)
+                att[128 * c:128 * c + 128, col:col + 256] = out[:, at:at + 128].T.astype(BF)
+
+    def send_state(state, out_to, lse_to, *names):
+        acc, m, l = state
+        out_to[...] = (acc / l).astype(BF)
+        lse_to[...] = jnp.broadcast_to(m + jnp.log(l), lse_to.shape)
+        start(*names)
+
+    def hold(state):
+        acc, m, l = state
+        st_acc[...] = acc
+        st_ml[0:8] = jnp.broadcast_to(m, (8, 512))
+        st_ml[8:16] = jnp.broadcast_to(l, (8, 512))
+
+    @pl.when(s == 0)
+    def _():
+        for g in (0, 1):
+            put(g, attend(rq[g], [own(g)], True), (0, 1))
+
+    @pl.when(s == 1)
+    def _():
+        recv(Q2B_1, V0B_1, K0B_1)
+        for c in (0, 1):
+            state = attend(rq2[256 * c:256 * c + 256, :], [first(1), own(1)], False)
+            send_state(state, s_c.at[0, c], t_c.at[0, c], OB_0 + c, LB_0 + c)
+        recv(Q3B_1)
+        for c in (0, 1):
+            state = attend(rq3[1, 256 * c:256 * c + 256, :], [first(1), own(1)], False)
+            send_state(state, s_c.at[1, c], t_c.at[1, c], OC_0 + c, LC_0 + c)
+        put(1, attend(rq[1], [first(1), own(1)], True), (0, 1))
+        recv(V0A_1, K0A_1)
+        put(0, attend(rq[0], [first(0), own(0)], True), (0, 1))
+
+    @pl.when(s == 2)
+    def _():
+        hold(attend(rq[1], [own(1)], True))
+        recv(Q3A_2, Q3B_2)
+        send_state(attend(rq3[1], [own(1)], False), s_b2, t_b2, O3B, L3B)
+        recv(V0A_2, K0A_2, V1A_2, K1A_2)
+        send_state(attend(rq3[0], [first(0), second(), own(0)], False), s_a, t_a, O3A, L3A)
+        put(0, attend(rq[0], [first(0), second(), own(0)], True), (0, 1))
+
+    @pl.when(s == 3)
+    def _():
+        state = attend(rq[1], [own(1)], True)
+        recv(O3B, L3B)
+        hold(merge(state, o_b2[...], l_b2[0:1]))
+        state = attend(rq[0], [own(0)], True)
+        recv(O3A, L3A)
+        put(0, merge(state, o_a[...], l_a[0:1]), (0, 1))
+
+    def x_copy(src, dst, i, dev):
+        return pltpu.make_async_remote_copy(
+            src_ref=src, dst_ref=dst, send_sem=xs.at[i], recv_sem=xr.at[i],
+            device_id={"tensor": dev}, device_id_type=MESH)
+
+    direction = dir_ref[...]
+    scale = 1.0 / jnp.sqrt(jnp.sum(direction * direction, axis=1, keepdims=True) + 1e-06)
+
+    def dir_half(x):
+        return dir_ref[:, pl.ds(pl.multiple_of(x * half, 128), half)] * scale
+
+    unit_halves = [dir_half(x_other), dir_half(x_here)]
+    local_dir = jnp.where(core == 0, unit_halves[1][:, :width], unit_halves[1][:, width:])
+    first_core = core == 0
+    waits = []
+    a_copies, b_copies, al_copies = {}, {}, {}
+    for c in (0, 1):
+        rows = slice(128 * c, 128 * c + 128)
+
+        @pl.when(s >= 2)
+        def _(c=c):
+            recv(OB_0 + c, LB_0 + c)
+            lanes = slice(256 * c, 256 * c + 256)
+            state = (st_acc[:, lanes], st_ml[0:1, lanes], st_ml[8:9, lanes])
+            put(1, merge(state, o_b1[c], l_b1[c, 0:1]), (c,))
+
+        dots = 0.0
+        for i in (0, 1):
+            if c == 0:
+                w_copies[i].wait()
+            part = jnp.dot(att[rows, :], wbuf[i], preferred_element_type=F32)
+            dots = dots + jnp.sum(part * unit_halves[i], axis=1, keepdims=True)
+            low, high = part[:, :width], part[:, width:]
+            a_send[c, i] = jnp.where(first_core, high, low).astype(BF)
+            a_copies[c, i] = x_copy(a_send.at[c, i], a_recv.at[c, i], 2 * c + i, core_peer)
+            a_copies[c, i].start()
+            keep[i, rows, :] = jnp.where(first_core, low, high)
+        a_copies[c, 0].wait_recv()
+        b_send[c] = (keep[0, rows, :] + a_recv[c, 0].astype(F32)).astype(BF)
+        b_copies[c] = x_copy(b_send.at[c], b_recv.at[c], 4 + c, x_peer)
+        b_copies[c].start()
+        dots = dots + jnp.sum(res_ref[rows, :].astype(F32) * local_dir, axis=1, keepdims=True)
+        al_send[c] = jnp.broadcast_to(dots, (128, 128)).T[0:8]
+        for j in (1, 2, 3):
+            i = 3 * c + j - 1
+            al_copies[c, j] = pltpu.make_async_remote_copy(
+                src_ref=al_send.at[c], dst_ref=al_recv.at[c, j - 1],
+                send_sem=als.at[i], recv_sem=alr.at[i],
+                device_id={"tensor": (t + j) % 4}, device_id_type=MESH)
+            al_copies[c, j].start()
+
+    for c in (0, 1):
+        rows = slice(128 * c, 128 * c + 128)
+        along = al_send[c]
+        for j in (1, 2, 3):
+            al_copies[c, j].wait_recv()
+            along = along + al_recv[c, j - 1]
+        along = jnp.broadcast_to(along[0:1], (128, 128)).T[:, 0:1]
+        a_copies[c, 1].wait_recv()
+        hidden = res_ref[rows, :].astype(F32) + keep[1, rows, :] + a_recv[c, 1].astype(F32)
+        hidden = hidden - along * local_dir
+        b_copies[c].wait_recv()
+        out_ref[rows, :] = (hidden + b_recv[c].astype(F32)).astype(BF)
+
+    for c in (0, 1):
+        a_copies[c, 0].wait_send()
+        a_copies[c, 1].wait_send()
+        b_copies[c].wait_send()
+        for j in (1, 2, 3):
+            al_copies[c, j].wait_send()
+
+    @pl.when(s == 0)
+    def _():
+        sent(V0A_2, K0A_2, V0B_1, K0B_1, V0A_1, K0A_1)
+
+    @pl.when(s == 1)
+    def _():
+        sent(V1A_2, K1A_2, OB_0, OB_1, LB_0, LB_1, OC_0, OC_1, LC_0, LC_1)
+
+    @pl.when(s == 2)
+    def _():
+        sent(Q2B_1, O3A, L3A, O3B, L3B)
+
+    @pl.when(s == 3)
+    def _():
+        sent(Q3B_1, Q3A_2, Q3B_2)
+
+
+def fused_body(queries, key_rows, value_rows, positions, residual, direction, out_weight):
+    cos, sin = rotary_tables(positions, HD)
+    cos, sin = cos[:, 0, :], sin[:, 0, :]
+    width = residual.shape[1]
+    vmem = pl.BlockSpec(memory_space=pltpu.VMEM)
+    dma = pltpu.SemaphoreType.DMA
+    return pl.pallas_call(
+        kernel,
+        out_shape=jax.ShapeDtypeStruct(residual.shape, BF),
+        in_specs=[vmem] * 7 + [pl.BlockSpec(memory_space=pl.ANY)],
+        out_specs=vmem,
+        scratch_shapes=[
+            pltpu.VMEM((2, out_weight.shape[0], 2 * width), BF),
+            pltpu.VMEM((2, 512, 256), BF),
+            pltpu.VMEM((2, 256, 256), BF),
+            pltpu.VMEM((4, 256, 256), BF),
+            pltpu.VMEM((2, 256, 256), BF),
+            pltpu.VMEM((2, 512, 256), BF),
+            pltpu.VMEM((512, 256), BF),
+            pltpu.VMEM((256, 512), BF),
+            pltpu.VMEM((256, 512), BF),
+            pltpu.VMEM((2, 256, 256), BF),
+            pltpu.VMEM((8, 512), F32),
+            pltpu.VMEM((8, 512), F32),
+            pltpu.VMEM((2, 8, 256), F32),
+            pltpu.VMEM((256, 512), BF),
+            pltpu.VMEM((256, 512), BF),
+            pltpu.VMEM((2, 2, 256, 256), BF),
+            pltpu.VMEM((8, 512), F32),
+            pltpu.VMEM((8, 512), F32),
+            pltpu.VMEM((2, 2, 8, 256), F32),
+            pltpu.VMEM((256, 512), F32),
+            pltpu.VMEM((16, 512), F32),
+            pltpu.VMEM((256, 1024), BF),
+            pltpu.VMEM((2, 256, width), F32),
+            pltpu.VMEM((2, 2, 128, width), BF),
+            pltpu.VMEM((2, 2, 128, width), BF),
+            pltpu.VMEM((2, 128, width), BF),
+            pltpu.VMEM((2, 128, width), BF),
+            pltpu.VMEM((2, 8, 128), F32),
+            pltpu.VMEM((2, 3, 8, 128), F32),
+            dma((SEQ_COPIES,)),
+            dma((SEQ_COPIES,)),
+            dma((2,)),
+            dma((6,)),
+            dma((6,)),
+            dma((6,)),
+            dma((6,)),
+        ],
+        compiler_params=pltpu.CompilerParams(
+            collective_id=0, has_side_effects=True, vmem_limit_bytes=48 * 1024 * 1024
+        ),
+    )(queries, key_rows, value_rows, cos, sin, residual, direction[None, :], out_weight)
+
+
+def device_body(*args):
+    queries, key_rows, _, _, residual, direction, _ = args
+    fits = (
+        lax.axis_size("seq") == 4
+        and lax.axis_size("tensor") == 4
+        and queries.shape == (256, 1024)
+        and key_rows.shape == (256, 512)
+        and residual.shape[1] * 4 == direction.shape[0]
+        and residual.shape[1] % 64 == 0
+        and WINDOW == 1024
+    )
+    return fused_body(*args) if fits else body(*args)
+
+
 def solution(mesh):
     return jax.shard_map(
-        body,
+        device_body,
         mesh=mesh,
         in_specs=(
             P(("groups", "seq"), "tensor"),

time: 119 us -> 64.4 us (0.54); the launches traced: 117 us -> 64.1 us
  waiting for transfers between devices: 59.4 us -> 0 us
  Pallas kernels: 0 us -> 56.9 us
  between operations: 14.4 us -> 0.04 us
  matrix products: 12.8 us -> 0 us
  starting transfers between devices: 9.89 us -> 0 us
  other arithmetic: 8.23 us -> 1.22 us
  blocking collectives: 5.51 us -> 0 us
    pallas_call x0 -> x1, Pallas kernels: none -> 56.9 us  [fused_body(): pl.pallas_call(kernel, out_shape=jax.ShapeDtypeStruct(residual.shape, BF)...]
    ppermute x8 -> x0, waiting for transfers between devices: 33.6 us -> none  [shifted_2(): lax.ppermute(value, axis, [(source, source + steps) for source in range(f...]
    unnamed x2 -> x0, waiting for transfers between devices: 25.8 us -> none
    dot_general x4 -> x0, matrix products: 12.8 us -> none  [the longest x1 5.74 us: body(): jnp.dot(attended, out_weight, preferred_element_type=jnp.float32)]
    ppermute x8 -> x0, starting transfers between devices: 9.89 us -> none  [shifted_2(): lax.ppermute(value, axis, [(source, source + steps) for source in range(f...]
    psum x1 -> x0, blocking collectives: 5.51 us -> none  [body(): along = lax.psum(dot_terms, 'tensor')]
    convert_element_type x3 -> x0, other arithmetic: 2.1 us -> none  [the longest x1 2.01 us: body(): (hidden_state - along[:, None] * local_dir[None, :]).astype(jnp.bfloat16)]
    sub x3 -> x0, other arithmetic: 1.78 us -> none  [the longest x1 1.59 us: body(): shifted = jnp.exp(scores - row_max)]
  transfers between devices with their start and end apart: 9 -> 0, of which waited for: 4 -> 0; matrix products, arithmetic and copies ran while one was open for 7% -> 0% of each run, Pallas kernels for 0% -> 0%
where the time goes in v1:
time: 64.4 us; the launch traced here: 64.1 us
  Pallas kernels  56.9 us (88%)
  local copies, waits for them, and re-layouts  5.89 us (9%)
  other arithmetic  1.22 us (2%)
    pallas_call x1, Pallas kernels, fused_body(): pl.pallas_call(kernel, out_shape=jax.ShapeDtypeStruct(residual.shape, BF)...  56.9 us
    unnamed x7, local copies, waits for them, and re-layouts  4.17 us

profile of v1, /device:TPU:25, one launch (start us, length us, event | category | flops | bytes accessed | tf_op | source)
XLA Modules:
  0.0 64.1 jit_solution(10987368859303553170)
XLA Ops:
  0.0 0.7 %convert_element_type.3 = f32[256]{0:T(256)S(1)} convert(s32[256]{0:T(256)} %param.10) | non-fusion elementwise | flops 256 | bytes 2048 | tf_op jit(solution)/shard_map/convert_element_type | solution.py:26
  0.7 0.7 %broadcast_in_dim.2.dir_ref = f32[1,3840]{1,0:T(1,128)S(1)} reshape(f32[3840]{0:T(1024)} %param.12) | data formatting | bytes 30720 | tf_op jit(solution)/shard_map/broadcast_in_dim | solution.py:473
  1.4 0.5 multiply_sine_fusion
  2.0 1.2 %copy.8.res_ref = bf16[256,960]{1,0:T(8,128)(2,1)S(1)} copy(bf16[256,960]{0,1:T(8,128)(2,1)} %param.11) | data formatting | bytes 983040 | tf_op args[4]
  3.2 0.0 copy-start
  3.2 1.0 %copy-done = bf16[256,1024]{1,0:T(8,128)(2,1)S(1)} copy-done((bf16[256,1024]{1,0:T(8,128)(2,1)S(1)}, bf16[256,1024]{1,0:T(8,128)(2,1)}, u32[]{:S(2)}) %copy-start) | copy-done | bytes 524312
  4.3 0.0 copy-start.1
  4.3 0.9 %copy-done.1 = bf16[256,512]{1,0:T(8,128)(2,1)S(1)} copy-done((bf16[256,512]{1,0:T(8,128)(2,1)S(1)}, bf16[256,512]{1,0:T(8,128)(2,1)}, u32[]{:S(2)}) %copy-start.1) | copy-done | bytes 262168
  5.2 0.0 copy-start.2
  5.2 0.9 %copy-done.2 = bf16[256,512]{1,0:T(8,128)(2,1)S(1)} copy-done((bf16[256,512]{1,0:T(8,128)(2,1)S(1)}, bf16[256,512]{1,0:T(8,128)(2,1)}, u32[]{:S(2)}) %copy-start.2) | copy-done | bytes 262168
  6.2 56.9 %shard_map.73 = bf16[256,960]{1,0:T(8,128)(2,1)S(1)} custom-call(bf16[256,1024]{1,0:T(8,128)(2,1)S(1)} %copy-done, bf16[256,512]{1,0:T(8,128)(2,1)S(1)} %copy-done.1, bf16[256,512]{1,0:T(8,128)(2,1)S(1)} %copy-done.2, f32[256,128]{1,0:T(8,128)S(1)} %get-tuple-element.6.cos_ref, f32[256,128]{1,0:T(8,128)S(1)} %get-tuple-element.5.sin_ref, ...), custom_call_target="tpu_custom_call" | custom-call | tf_op jit(solution)/shard_map/pallas_call | solution.py:427
  63.1 1.0 %copy.9 = bf16[256,960]{0,1:T(8,128)(2,1)} copy(bf16[256,960]{1,0:T(8,128)(2,1)S(1)} %shard_map.73) | data formatting | bytes 983040 | tf_op jit(solution)/shard_map/pallas_call | solution.py:427
  (1 shorter events, 0.0 us)
Async XLA Ops:
  3.2 1.0 %copy-start = (bf16[256,1024]{1,0:T(8,128)(2,1)S(1)}, bf16[256,1024]{1,0:T(8,128)(2,1)}, u32[]{:S(2)}) copy-start(bf16[256,1024]{1,0:T(8,128)(2,1)} %q_ref.1) | copy-start | bytes 1572868
  4.3 0.9 %copy-start.1 = (bf16[256,512]{1,0:T(8,128)(2,1)S(1)}, bf16[256,512]{1,0:T(8,128)(2,1)}, u32[]{:S(2)}) copy-start(bf16[256,512]{1,0:T(8,128)(2,1)} %k_ref.1) | copy-start | bytes 786436
  5.2 0.9 %copy-start.2 = (bf16[256,512]{1,0:T(8,128)(2,1)S(1)}, bf16[256,512]{1,0:T(8,128)(2,1)}, u32[]{:S(2)}) copy-start(bf16[256,512]{1,0:T(8,128)(2,1)} %v_ref.1) | copy-start | bytes 786436

commit v2 on v1

v2 whole, which is shorter than its diff:
```python
import functools

import jax
import jax.numpy as jnp
from jax import lax
from jax.experimental import pallas as pl
from jax.experimental.pallas import tpu as pltpu
from jax.sharding import PartitionSpec as P

HD = 256
WINDOW = 1024


big_negative = -1e30


def shifted_2(value, axis, steps):
    count = lax.axis_size(axis)
    first, last = (max(0, -steps), min(count, count - steps))
    return lax.ppermute(value, axis, [(source, source + steps) for source in range(first, last)])


def rotary_tables(positions, head_dim):
    half_dim = head_dim // 2
    freqs = jnp.power(10000.0, -jnp.arange(half_dim, dtype=jnp.float32) * 2.0 / head_dim)
    angles = positions.astype(jnp.float32)[:, None] * freqs[None, :]
    return (jnp.cos(angles)[:, None, :], jnp.sin(angles)[:, None, :])


def rotate_heads(block, cos_table, sin_table, head_dim):
    row_count = block.shape[0]
    head_count = block.shape[1] // head_dim
    half_dim = head_dim // 2
    widened = block.reshape(row_count, head_count, head_dim).astype(jnp.float32)
    first_half = widened[:, :, :half_dim]
    second_half = widened[:, :, half_dim:]
    turned = jnp.concatenate(
        [
            first_half * cos_table - second_half * sin_table,
            second_half * cos_table + first_half * sin_table,
        ],
        axis=-1,
    )
    return turned.reshape(row_count, head_count * head_dim)


def body(queries, key_rows, value_rows, positions, residual, direction, out_weight):
    tokens_here = queries.shape[0]
    query_heads = queries.shape[1] // HD
    kv_heads = key_rows.shape[1] // HD
    group_size = query_heads // kv_heads
    span_blocks = WINDOW // tokens_here
    seq_index = lax.axis_index("seq")
    cos_table, sin_table = rotary_tables(positions, HD)
    rot_queries = (rotate_heads(queries, cos_table, sin_table, HD) * HD ** (-0.5)).astype(
        jnp.bfloat16
    )
    rot_keys = rotate_heads(key_rows, cos_table, sin_table, HD).astype(jnp.bfloat16)
    query_blocks = rot_queries.reshape(tokens_here, kv_heads, group_size, HD)
    own_scores = jnp.einsum(
        "qkgd,skd->kgqs",
        query_blocks,
        rot_keys.reshape(tokens_here, kv_heads, HD),
        preferred_element_type=jnp.float32,
    )
    earlier_keys = []
    earlier_values = []
    for distance in range(span_blocks, 0, -1):
        moved_keys, moved_values = shifted_2((rot_keys, value_rows), "seq", distance)
        earlier_keys.append(moved_keys)
        earlier_values.append(moved_values)
    far_keys = jnp.concatenate(earlier_keys, axis=0)
    far_values = jnp.concatenate(earlier_values, axis=0)
    far_scores = jnp.einsum(
        "qkgd,skd->kgqs",
        query_blocks,
        far_keys.reshape(-1, kv_heads, HD),
        preferred_element_type=jnp.float32,
    )
    scores = jnp.concatenate([far_scores, own_scores], axis=-1)
    query_index = seq_index * tokens_here + jnp.arange(tokens_here, dtype=jnp.int32)
    key_index = (seq_index - span_blocks) * tokens_here + jnp.arange(
        (span_blocks + 1) * tokens_here, dtype=jnp.int32
    )
    gap_grid = query_index[:, None] - key_index[None, :]
    allowed = (gap_grid >= 0) & (gap_grid < WINDOW) & (key_index[None, :] >= 0)
    scores = jnp.where(allowed, scores, big_negative)
    row_max = jnp.max(scores, axis=-1, keepdims=True)
    shifted = jnp.exp(scores - row_max)
    row_sum = jnp.sum(shifted, axis=-1, keepdims=True)
    weights = (shifted / row_sum).astype(jnp.bfloat16)
    every_value = jnp.concatenate([far_values, value_rows], axis=0).reshape(-1, kv_heads, HD)
    mixed = jnp.einsum("kgqs,skd->qkgd", weights, every_value, preferred_element_type=jnp.float32)
    attended = mixed.astype(jnp.bfloat16).reshape(tokens_here, query_heads * HD)
    partial_value = jnp.dot(attended, out_weight, preferred_element_type=jnp.float32)
    unit_dir = direction / jnp.sqrt(jnp.sum(direction * direction) + 1e-06)
    column_width = residual.shape[1]
    tensor_index = lax.axis_index("tensor")
    local_dir = lax.dynamic_slice_in_dim(unit_dir, tensor_index * column_width, column_width, 0)
    base_state = residual.astype(jnp.float32)
    rounded_terms = partial_value.astype(jnp.bfloat16).astype(jnp.float32)
    dot_terms = jnp.sum(rounded_terms * unit_dir[None, :], axis=1) + jnp.sum(
        base_state * local_dir[None, :], axis=1
    )
    along = lax.psum(dot_terms, "tensor")
    summed = lax.psum_scatter(
        partial_value.astype(jnp.bfloat16), "tensor", scatter_dimension=1, tiled=True
    ).astype(jnp.float32)
    hidden_state = base_state + summed
    ablated = (hidden_state - along[:, None] * local_dir[None, :]).astype(jnp.bfloat16)
    return ablated


BF = jnp.bfloat16
F32 = jnp.float32
MESH = pl.DeviceIdType.MESH

def rot(x, cos, sin):
    x = x.astype(F32)
    a, b = x[:, :128], x[:, 128:]
    return jnp.concatenate([a * cos - b * sin, b * cos + a * sin], axis=1)


def attend(q, blocks, diag):
    scores = [
        lax.dot_general(k, q, (((1,), (1,)), ((), ())), preferred_element_type=F32)
        for k, _ in blocks
    ]
    if diag:
        s = scores[-1]
        key = lax.broadcasted_iota(jnp.int32, s.shape, 0)
        lane = lax.broadcasted_iota(jnp.int32, s.shape, 1)
        row = (lane // 256) * 128 + lane % 128
        scores[-1] = jnp.where(key <= row, s, big_negative)
    m = functools.reduce(jnp.maximum, [jnp.max(s, axis=0, keepdims=True) for s in scores])
    acc, l = 0.0, 0.0
    for s, (_, v) in zip(scores, blocks):
        p = jnp.exp(s - m)
        l = l + jnp.sum(p, axis=0, keepdims=True)
        acc = acc + lax.dot_general(
            v, p.astype(BF), (((0,), (0,)), ((), ())), preferred_element_type=F32
        )
    return acc, m, l


def merge(state, out, lse):
    acc, m, l = state
    top = jnp.maximum(m, lse)
    mine, other = jnp.exp(m - top), jnp.exp(lse - top)
    return acc * mine + out.astype(F32) * other, top, l * mine + other


def kernel(pos_hbm, freq_ref, q_hbm, k_hbm, v_hbm, res_hbm, dir_hbm, w_hbm, out_ref,
           pos, direction, q, k, v, res, wbuf, wt, ucol, rq, rk, kv0, kv1, rq3, rq2,
           o_a, o_b2, o_b1, l_a, l_b2, l_b1, s_a, s_b2, s_c, t_a, t_b2, t_c,
           st_acc, st_ml, att, keep, a_send, a_recv, b_send, b_recv, al_send, al_recv,
           lsem, ssem, rsem, xs, xr, als, alr):
    s = lax.axis_index("seq")
    t = lax.axis_index("tensor")
    core = t % 2
    x_here = t // 2
    x_other = 1 - x_here
    core_peer = t + 1 - 2 * core
    x_peer = (t + 2) % 4
    half = wbuf.shape[2]
    width = half // 2

    local = {}

    def fetch(name, src, dst):
        local[name] = pltpu.make_async_copy(src, dst, lsem.at[len(local)])
        local[name].start()

    fetch("pos", pos_hbm, pos)
    fetch("k", k_hbm, k)
    fetch("q", q_hbm, q)
    fetch("v", v_hbm, v)
    for i, x in enumerate((x_other, x_here)):
        cols = pl.ds(pl.multiple_of(x * half, 128), half)
        fetch(i, w_hbm.at[:, cols], wbuf.at[i])
    fetch("dir", dir_hbm, direction)
    fetch("res", res_hbm, res)

    barrier = pltpu.get_barrier_semaphore()
    for j in (1, 2, 3):
        pl.semaphore_signal(barrier, inc=1, device_id={"seq": (s + j) % 4}, device_id_type=MESH)
        pl.semaphore_signal(barrier, inc=1, device_id={"tensor": (t + j) % 4}, device_id_type=MESH)
    pl.semaphore_wait(barrier, 6)

    copies, index = {}, {}

    def add(name, dev, src, dst, lands_as=None):
        i = index[name] = len(index)
        copies[name] = pltpu.make_async_remote_copy(
            src_ref=src, dst_ref=dst, send_sem=ssem.at[i],
            recv_sem=rsem.at[i if lands_as is None else index[lands_as]],
            device_id={"seq": dev}, device_id_type=MESH)

    for g, name in ((0, "a"), (1, "b")):
        cols = slice(256 * g, 256 * g + 256)
        add("v0" + name + "1", 1, v_hbm.at[:, cols], kv0.at[2 * g + 1])
        add("k0" + name + "1", 1, rk.at[g], kv0.at[2 * g])
    add("v0a2", 2, v_hbm.at[:, 0:256], kv0.at[1])
    add("k0a2", 2, rk.at[0], kv0.at[0])
    add("v1a2", 2, v_hbm.at[:, 0:256], kv1.at[1])
    add("k1a2", 2, rk.at[0], kv1.at[0])
    add("q3a2", 2, rq.at[0], rq3.at[0])
    add("o3b", 3, s_b2, o_b2)
    add("l3b", 3, t_b2, l_b2)
    for c in (0, 1):
        rows = slice(256 * c, 256 * c + 256)
        n = str(c)
        add("q3b2" + n, 2, rq.at[1, rows], rq3.at[1, rows])
        add("f3b1" + n, 1, rq3.at[1, rows], rq3.at[1, rows])
        add("q2b1" + n, 1, rq.at[1, rows], rq2.at[rows])
        add("o3a" + n, 3, s_a.at[c], o_a.at[c])
        add("l3a" + n, 3, t_a.at[c], l_a.at[c])
        add("o2b" + n, 2, s_c.at[0, c], o_b1.at[c])
        add("l2b" + n, 2, t_c.at[0, c], l_b1.at[c])
        add("o3c" + n, 3, s_c.at[1, c], o_b1.at[c], "o2b" + n)
        add("l3c" + n, 3, t_c.at[1, c], l_b1.at[c], "l2b" + n)

    def start(*names):
        for n in names:
            copies[n].start()

    def recv(*names):
        for n in names:
            copies[n].wait_recv()

    def sent(*names):
        for n in names:
            copies[n].wait_send()

    @pl.when(s == 0)
    def _():
        start("v0b1")

    @pl.when(s == 1)
    def _():
        start("v1a2")

    local["pos"].wait()
    freqs = freq_ref[...]
    tokens = pos[...].astype(F32).reshape(1, 256)
    angles = jnp.concatenate(
        [jnp.broadcast_to(tokens[:, 128 * c:128 * c + 128], (128, 128)).T for c in (0, 1)], axis=0
    ) * freqs
    cos, sin = jnp.cos(angles), jnp.sin(angles)
    local["k"].wait()
    for g in (1, 0):
        rk[g] = rot(k[:, 256 * g:256 * g + 256], cos, sin).astype(BF)

    @pl.when(s == 0)
    def _():
        start("k0b1")

    @pl.when(s == 1)
    def _():
        start("k1a2")

    local["q"].wait()
    for g in (1, 0):
        for h in (0, 1):
            at = 256 * (2 * g + h)
            r = (rot(q[:, at:at + 256], cos, sin) * HD ** (-0.5)).astype(BF)
            for c in (0, 1):
                rq[g, 256 * c + 128 * h:256 * c + 128 * h + 128, :] = r[128 * c:128 * c + 128]
        if g == 1:
            @pl.when(s == 3)
            def _():
                start("q3b20")

            @pl.when(s == 2)
            def _():
                start("q2b10")

    local["v"].wait()

    def own(g):
        return rk[g], v[:, 256 * g:256 * g + 256]

    def first(g):
        return kv0[2 * g], kv0[2 * g + 1]

    def second():
        return kv1[0], kv1[1]

    def put(g, state, chunks):
        acc, _, l = state
        out = (acc / l).astype(BF)
        for i, c in enumerate(chunks):
            for h in (0, 1):
                at = 256 * i + 128 * h
                row = 256 * (2 * g + h)
                att[c, row:row + 256, :] = out[:, at:at + 128]

    def send_state(state, out_to, lse_to, *names):
        acc, m, l = state
        out_to[...] = (acc / l).astype(BF)
        lse_to[...] = jnp.broadcast_to(m + jnp.log(l), lse_to.shape)
        start(*names)

    def hold(g, state):
        acc, m, l = state
        st_acc[g] = acc
        st_ml[g, 0:8] = jnp.broadcast_to(m, (8, 512))
        st_ml[g, 8:16] = jnp.broadcast_to(l, (8, 512))

    def held(g, c):
        lanes = slice(256 * c, 256 * c + 256)
        return st_acc[g, :, lanes], st_ml[g, 0:1, lanes], st_ml[g, 8:9, lanes]

    def prepare_weight():
        local["dir"].wait()
        whole = direction[...].reshape(1, 2 * half)
        scale = 1.0 / jnp.sqrt(jnp.sum(whole * whole, axis=1, keepdims=True) + 1e-06)
        for i, x in enumerate((x_other, x_here)):
            local[i].wait()
            mine = jnp.where(x == 0, whole[:, :half], whole[:, half:]) * scale
            for j in range(half // 128):
                at = slice(128 * j, 128 * j + 128)
                wt[i, at, :] = wbuf[i, :, at].T
                ucol[i, at, :] = jnp.broadcast_to(mine[:, at], (128, 128)).T

    @pl.when(s == 0)
    def _():
        put(1, attend(rq[1], [own(1)], True), (0, 1))
        sent("v0b1")
        start("v0a2")
        put(0, attend(rq[0], [own(0)], True), (0, 1))
        sent("k0b1")
        start("k0a2")

    @pl.when(s == 2)
    def _():
        recv("q3b20")
        start("f3b10")
        sent("q2b10")
        start("q2b11")
        hold(1, attend(rq[1], [own(1)], True))
        recv("q3b21")
        start("f3b11")
        send_state(attend(rq3[1], [own(1)], False), s_b2, t_b2, "o3b", "l3b")

    @pl.when(s == 3)
    def _():
        sent("q3b20")
        start("q3b21")
        hold(0, attend(rq[0], [own(0)], True))
        sent("q3b21")
        start("q3a2")
        hold(1, attend(rq[1], [own(1)], True))

    prepare_weight()

    @pl.when(s == 0)
    def _():
        sent("v0a2")
        start("v0a1")
        sent("k0a2")
        start("k0a1")

    @pl.when(s == 1)
    def _():
        recv("v0b1", "k0b1")
        for c in (0, 1):
            n = str(c)
            rows = slice(256 * c, 256 * c + 256)
            recv("q2b1" + n)
            state = attend(rq2[rows, :], [first(1), own(1)], False)
            send_state(state, s_c.at[0, c], t_c.at[0, c], "o2b" + n, "l2b" + n)
            recv("f3b1" + n)
            state = attend(rq3[1, rows, :], [first(1), own(1)], False)
            send_state(state, s_c.at[1, c], t_c.at[1, c], "o3c" + n, "l3c" + n)
        put(1, attend(rq[1], [first(1), own(1)], True), (0, 1))
        recv("v0a1", "k0a1")
        put(0, attend(rq[0], [first(0), own(0)], True), (0, 1))

    @pl.when(s == 2)
    def _():
        recv("v1a2", "k1a2", "q3a2", "v0a2", "k0a2")
        for c in (0, 1):
            n = str(c)
            rows = slice(256 * c, 256 * c + 256)
            state = attend(rq3[0, rows, :], [first(0), second(), own(0)], False)
            send_state(state, s_a.at[c], t_a.at[c], "o3a" + n, "l3a" + n)
        put(0, attend(rq[0], [first(0), second(), own(0)], True), (0, 1))

    @pl.when(s == 3)
    def _():
        recv("o3b", "l3b")
        acc, m, l = st_acc[1], st_ml[1, 0:1], st_ml[1, 8:9]
        hold(1, merge((acc, m, l), o_b2[...], l_b2[0:1]))

    def x_copy(src, dst, i, dev):
        return pltpu.make_async_remote_copy(
            src_ref=src, dst_ref=dst, send_sem=xs.at[i], recv_sem=xr.at[i],
            device_id={"tensor": dev}, device_id_type=MESH)

    local["res"].wait()
    first_core = core == 0
    local_dir = jnp.where(first_core, ucol[1, :width], ucol[1, width:])
    a_copies, b_copies, al_copies = {}, {}, {}
    for c in (0, 1):
        lanes = slice(128 * c, 128 * c + 128)

        @pl.when(s == 3)
        def _(c=c):
            recv("o3a" + str(c), "l3a" + str(c))
            put(0, merge(held(0, c), o_a[c], l_a[c, 0:1]), (c,))

        @pl.when(s >= 2)
        def _(c=c):
            recv("o2b" + str(c), "l2b" + str(c))
            put(1, merge(held(1, c), o_b1[c], l_b1[c, 0:1]), (c,))

        dots = jnp.sum(res[:, lanes].astype(F32) * local_dir, axis=0, keepdims=True)
        for i in (0, 1):
            part = jnp.dot(wt[i], att[c], preferred_element_type=F32)
            dots = dots + jnp.sum(part * ucol[i], axis=0, keepdims=True)
            low, high = part[:width], part[width:]
            a_send[c, i] = jnp.where(first_core, high, low).astype(BF)
            a_copies[c, i] = x_copy(a_send.at[c, i], a_recv.at[c, i], 2 * c + i, core_peer)
            a_copies[c, i].start()
            keep[c, i] = jnp.where(first_core, low, high)
            if i == 0:
                a_copies[c, 0].wait_recv()
                b_send[c] = (keep[c, 0] + a_recv[c, 0].astype(F32)).astype(BF)
                b_copies[c] = x_copy(b_send.at[c], b_recv.at[c], 4 + c, x_peer)
                b_copies[c].start()
        al_send[c] = jnp.broadcast_to(dots, (8, 128))
        for j in (1, 2, 3):
            i = 3 * c + j - 1
            al_copies[c, j] = pltpu.make_async_remote_copy(
                src_ref=al_send.at[c], dst_ref=al_recv.at[c, j - 1],
                send_sem=als.at[i], recv_sem=alr.at[i],
                device_id={"tensor": (t + j) % 4}, device_id_type=MESH)
            al_copies[c, j].start()

    for c in (0, 1):
        lanes = slice(128 * c, 128 * c + 128)
        along = al_send[c]
        for j in (1, 2, 3):
            al_copies[c, j].wait_recv()
            along = along + al_recv[c, j - 1]
        a_copies[c, 1].wait_recv()
        hidden = res[:, lanes].astype(F32) + keep[c, 1] + a_recv[c, 1].astype(F32)
        keep[c, 1] = hidden - along[0:1] * local_dir
        b_copies[c].wait_recv()
        out_ref[:, lanes] = (keep[c, 1] + b_recv[c].astype(F32)).astype(BF)

    for c in (0, 1):
        a_copies[c, 0].wait_send()
        a_copies[c, 1].wait_send()
        b_copies[c].wait_send()
        for j in (1, 2, 3):
            al_copies[c, j].wait_send()

    @pl.when(s == 0)
    def _():
        sent("v0a1", "k0a1")

    @pl.when(s == 1)
    def _():
        sent("v1a2", "k1a2", "o2b0", "l2b0", "o2b1", "l2b1", "o3c0", "l3c0", "o3c1", "l3c1")

    @pl.when(s == 2)
    def _():
        sent("q2b11", "f3b10", "f3b11", "o3b", "l3b", "o3a0", "l3a0", "o3a1", "l3a1")

    @pl.when(s == 3)
    def _():
        sent("q3a2")


def fused_body(queries, key_rows, value_rows, positions, residual, direction, out_weight):
    freqs = jnp.power(10000.0, -jnp.arange(HD // 2, dtype=F32) * 2.0 / HD)[None, :]
    rows, width = residual.shape
    depth = out_weight.shape[0]
    vmem = pl.BlockSpec(memory_space=pltpu.VMEM)
    anywhere = pl.BlockSpec(memory_space=pl.ANY)
    dma = pltpu.SemaphoreType.DMA
    out = pl.pallas_call(
        kernel,
        out_shape=jax.ShapeDtypeStruct((width, rows), BF),
        in_specs=[anywhere, vmem] + [anywhere] * 6,
        out_specs=vmem,
        scratch_shapes=[
            pltpu.VMEM(positions.shape, jnp.int32),
            pltpu.VMEM(direction.shape, F32),
            pltpu.VMEM(queries.shape, BF),
            pltpu.VMEM(key_rows.shape, BF),
            pltpu.VMEM(value_rows.shape, BF),
            pltpu.VMEM((width, rows), BF),
            pltpu.VMEM((2, depth, 2 * width), BF),
            pltpu.VMEM((2, 2 * width, depth), BF),
            pltpu.VMEM((2, 2 * width, 128), F32),
            pltpu.VMEM((2, 512, 256), BF),
            pltpu.VMEM((2, 256, 256), BF),
            pltpu.VMEM((4, 256, 256), BF),
            pltpu.VMEM((2, 256, 256), BF),
            pltpu.VMEM((2, 512, 256), BF),
            pltpu.VMEM((512, 256), BF),
            pltpu.VMEM((2, 256, 256), BF),
            pltpu.VMEM((256, 512), BF),
            pltpu.VMEM((2, 256, 256), BF),
            pltpu.VMEM((2, 8, 256), F32),
            pltpu.VMEM((8, 512), F32),
            pltpu.VMEM((2, 8, 256), F32),
            pltpu.VMEM((2, 256, 256), BF),
            pltpu.VMEM((256, 512), BF),
            pltpu.VMEM((2, 2, 256, 256), BF),
            pltpu.VMEM((2, 8, 256), F32),
            pltpu.VMEM((8, 512), F32),
            pltpu.VMEM((2, 2, 8, 256), F32),
            pltpu.VMEM((2, 256, 512), F32),
            pltpu.VMEM((2, 16, 512), F32),
            pltpu.VMEM((2, depth, 128), BF),
            pltpu.VMEM((2, 2, width, 128), F32),
            pltpu.VMEM((2, 2, width, 128), BF),
            pltpu.VMEM((2, 2, width, 128), BF),
            pltpu.VMEM((2, width, 128), BF),
            pltpu.VMEM((2, width, 128), BF),
            pltpu.VMEM((2, 8, 128), F32),
            pltpu.VMEM((2, 3, 8, 128), F32),
            dma((8,)),
            dma((29,)),
            dma((29,)),
            dma((6,)),
            dma((6,)),
            dma((6,)),
            dma((6,)),
        ],
        compiler_params=pltpu.CompilerParams(
            collective_id=0, has_side_effects=True, vmem_limit_bytes=60 * 1024 * 1024
        ),
    )(positions, freqs, queries, key_rows, value_rows, residual.T, direction, out_weight)
    return out.T


def device_body(*args):
    queries, key_rows, _, _, residual, direction, _ = args
    fits = (
        lax.axis_size("seq") == 4
        and lax.axis_size("tensor") == 4
        and queries.shape == (256, 1024)
        and key_rows.shape == (256, 512)
        and residual.shape[1] * 4 == direction.shape[0]
        and residual.shape[1] % 64 == 0
        and WINDOW == 1024
    )
    return fused_body(*args) if fits else body(*args)


def solution(mesh):
    return jax.shard_map(
        device_body,
        mesh=mesh,
        in_specs=(
            P(("groups", "seq"), "tensor"),
            P(("groups", "seq"), "tensor"),
            P(("groups", "seq"), "tensor"),
            P(("groups", "seq")),
            P(("groups", "seq"), "tensor"),
            P("groups"),
            P("tensor", None),
        ),
        out_specs=P(("groups", "seq"), "tensor"),
        check_vma=False,
    )
```

time: 64.4 us -> 48.5 us (0.75)
  the two profiles are of different devices: /device:TPU:25 before, /device:TPU:27 now
where the time goes in v2:
time: 48.5 us; the launch traced here: 48.3 us
  Pallas kernels  45.9 us (95%)
  local copies, waits for them, and re-layouts  1.84 us (4%)
  other arithmetic  0.52 us (1%)
    pallas_call x1, Pallas kernels, fused_body(): pl.pallas_call(kernel, out_shape=jax.ShapeDtypeStruct((width, rows), BF),...  45.9 us
    unnamed x1, local copies, waits for them, and re-layouts  1.84 us

profile of v2, /device:TPU:27, one launch (start us, length us, event | category | flops | bytes accessed | tf_op | source)
XLA Modules:
  0.0 48.3 jit_solution(13211222937278207095)
XLA Ops:
  0.0 0.5 %multiply_power_fusion.freq_ref = f32[1,128]{1,0:T(1,128)} fusion(), kind=kLoop, calls=%fused_computation | loop fusion | flops 256 | bytes 512 | tf_op jit(solution)/shard_map/pow | solution.py:478
  0.5 45.9 %shard_map.73 = bf16[960,256]{1,0:T(8,128)(2,1)} custom-call(s32[256]{0:T(256)} %pos_hbm.1, f32[1,128]{1,0:T(1,128)} %multiply_power_fusion.freq_ref, bf16[256,1024]{1,0:T(8,128)(2,1)} %q_hbm.1, bf16[256,512]{1,0:T(8,128)(2,1)} %k_hbm.1, bf16[256,512]{1,0:T(8,128)(2,1)} %v_hbm.1, bf16[960,256]{1,0:T(8,128)(2,1)} %bitcast.3, f32[3840]{0:T(1024)} %dir_hbm.1, ...), custom_call_target="tpu_custom_call" | custom-call | tf_op jit(solution)/shard_map/pallas_call | solution.py:484
  46.5 1.8 %copy.9 = bf16[256,960]{0,1:T(8,128)(2,1)} copy(bf16[256,960]{0,1:T(8,128)(2,1)} %bitcast.2) | data formatting | bytes 983040

commit v3 on v2

--- a/solution.py
+++ b/solution.py
@@ -234,7 +234,7 @@
 
     @pl.when(s == 0)
     def _():
-        start("v0b1")
+        start("v0b1", "v0a2")
 
     @pl.when(s == 1)
     def _():
@@ -253,7 +253,7 @@
 
     @pl.when(s == 0)
     def _():
-        start("k0b1")
+        start("k0b1", "k0a2")
 
     @pl.when(s == 1)
     def _():
@@ -326,11 +326,9 @@
     @pl.when(s == 0)
     def _():
         put(1, attend(rq[1], [own(1)], True), (0, 1))
-        sent("v0b1")
-        start("v0a2")
+        sent("v0b1", "v0a2")
+        start("v0a1", "k0a1")
         put(0, attend(rq[0], [own(0)], True), (0, 1))
-        sent("k0b1")
-        start("k0a2")
 
     @pl.when(s == 2)
     def _():
@@ -352,14 +350,9 @@
         start("q3a2")
         hold(1, attend(rq[1], [own(1)], True))
 
-    prepare_weight()
-
-    @pl.when(s == 0)
-    def _():
-        sent("v0a2")
-        start("v0a1")
-        sent("k0a2")
-        start("k0a1")
+    @pl.when(s != 1)
+    def _():
+        prepare_weight()
 
     @pl.when(s == 1)
     def _():
@@ -374,6 +367,7 @@
             state = attend(rq3[1, rows, :], [first(1), own(1)], False)
             send_state(state, s_c.at[1, c], t_c.at[1, c], "o3c" + n, "l3c" + n)
         put(1, attend(rq[1], [first(1), own(1)], True), (0, 1))
+        prepare_weight()
         recv("v0a1", "k0a1")
         put(0, attend(rq[0], [first(0), own(0)], True), (0, 1))
 
@@ -399,8 +393,9 @@
             device_id={"tensor": dev}, device_id_type=MESH)
 
     local["res"].wait()
-    first_core = core == 0
-    local_dir = jnp.where(first_core, ucol[1, :width], ucol[1, width:])
+    own_part = pl.ds(pl.multiple_of(core * width, 64), width)
+    peer_part = pl.ds(pl.multiple_of((1 - core) * width, 64), width)
+    local_dir = ucol[1, own_part, :]
     a_copies, b_copies, al_copies = {}, {}, {}
     for c in (0, 1):
         lanes = slice(128 * c, 128 * c + 128)
@@ -417,18 +412,20 @@
 
         dots = jnp.sum(res[:, lanes].astype(F32) * local_dir, axis=0, keepdims=True)
         for i in (0, 1):
-            part = jnp.dot(wt[i], att[c], preferred_element_type=F32)
-            dots = dots + jnp.sum(part * ucol[i], axis=0, keepdims=True)
-            low, high = part[:width], part[width:]
-            a_send[c, i] = jnp.where(first_core, high, low).astype(BF)
+            part = jnp.dot(wt[i, peer_part, :], att[c], preferred_element_type=F32)
+            a_send[c, i] = part.astype(BF)
             a_copies[c, i] = x_copy(a_send.at[c, i], a_recv.at[c, i], 2 * c + i, core_peer)
             a_copies[c, i].start()
-            keep[c, i] = jnp.where(first_core, low, high)
+            dots = dots + jnp.sum(part * ucol[i, peer_part, :], axis=0, keepdims=True)
+            part = jnp.dot(wt[i, own_part, :], att[c], preferred_element_type=F32)
             if i == 0:
                 a_copies[c, 0].wait_recv()
-                b_send[c] = (keep[c, 0] + a_recv[c, 0].astype(F32)).astype(BF)
+                b_send[c] = (part + a_recv[c, 0].astype(F32)).astype(BF)
                 b_copies[c] = x_copy(b_send.at[c], b_recv.at[c], 4 + c, x_peer)
                 b_copies[c].start()
+            else:
+                keep[c] = part
+            dots = dots + jnp.sum(part * ucol[i, own_part, :], axis=0, keepdims=True)
         al_send[c] = jnp.broadcast_to(dots, (8, 128))
         for j in (1, 2, 3):
             i = 3 * c + j - 1
@@ -445,10 +442,10 @@
             al_copies[c, j].wait_recv()
             along = along + al_recv[c, j - 1]
         a_copies[c, 1].wait_recv()
-        hidden = res[:, lanes].astype(F32) + keep[c, 1] + a_recv[c, 1].astype(F32)
-        keep[c, 1] = hidden - along[0:1] * local_dir
+        hidden = res[:, lanes].astype(F32) + keep[c] + a_recv[c, 1].astype(F32)
+        keep[c] = hidden - along[0:1] * local_dir
         b_copies[c].wait_recv()
-        out_ref[:, lanes] = (keep[c, 1] + b_recv[c].astype(F32)).astype(BF)
+        out_ref[:, lanes] = (keep[c] + b_recv[c].astype(F32)).astype(BF)
 
     for c in (0, 1):
         a_copies[c, 0].wait_send()
@@ -459,7 +456,7 @@
 
     @pl.when(s == 0)
     def _():
-        sent("v0a1", "k0a1")
+        sent("k0b1", "k0a2", "v0a1", "k0a1")
 
     @pl.when(s == 1)
     def _():
@@ -517,7 +514,7 @@
             pltpu.VMEM((2, 256, 512), F32),
             pltpu.VMEM((2, 16, 512), F32),
             pltpu.VMEM((2, depth, 128), BF),
-            pltpu.VMEM((2, 2, width, 128), F32),
+            pltpu.VMEM((2, width, 128), F32),
             pltpu.VMEM((2, 2, width, 128), BF),
             pltpu.VMEM((2, 2, width, 128), BF),
             pltpu.VMEM((2, width, 128), BF),

time: 48.5 us -> 46.6 us (0.961)
  the two profiles are of different devices: /device:TPU:27 before, /device:TPU:25 now
where the time goes in v3:
time: 46.6 us; the launch traced here: 46.4 us
  Pallas kernels  44.1 us (95%)
  local copies, waits for them, and re-layouts  1.84 us (4%)
  other arithmetic  0.52 us (1%)
    pallas_call x1, Pallas kernels, fused_body(): pl.pallas_call(kernel, out_shape=jax.ShapeDtypeStruct((width, rows), BF),...  44.1 us
    unnamed x1, local copies, waits for them, and re-layouts  1.84 us

profile of v3, /device:TPU:25, one launch (start us, length us, event | category | flops | bytes accessed | tf_op | source)
XLA Modules:
  0.0 46.4 jit_solution(10606661678947147743)
XLA Ops:
  0.0 0.5 %multiply_power_fusion.freq_ref = f32[1,128]{1,0:T(1,128)} fusion(), kind=kLoop, calls=%fused_computation | loop fusion | flops 256 | bytes 512 | tf_op jit(solution)/shard_map/pow | solution.py:475
  0.5 44.1 %shard_map.73 = bf16[960,256]{1,0:T(8,128)(2,1)} custom-call(s32[256]{0:T(256)} %pos_hbm.1, f32[1,128]{1,0:T(1,128)} %multiply_power_fusion.freq_ref, bf16[256,1024]{1,0:T(8,128)(2,1)} %q_hbm.1, bf16[256,512]{1,0:T(8,128)(2,1)} %k_hbm.1, bf16[256,512]{1,0:T(8,128)(2,1)} %v_hbm.1, bf16[960,256]{1,0:T(8,128)(2,1)} %bitcast.3, f32[3840]{0:T(1024)} %dir_hbm.1, ...), custom_call_target="tpu_custom_call" | custom-call | tf_op jit(solution)/shard_map/pallas_call | solution.py:481
  44.6 1.8 %copy.9 = bf16[256,960]{0,1:T(8,128)(2,1)} copy(bf16[256,960]{0,1:T(8,128)(2,1)} %bitcast.2) | data formatting | bytes 983040

commit v4 on v3

--- a/solution.py
+++ b/solution.py
@@ -151,9 +151,9 @@
 
 
 def kernel(pos_hbm, freq_ref, q_hbm, k_hbm, v_hbm, res_hbm, dir_hbm, w_hbm, out_ref,
-           pos, direction, q, k, v, res, wbuf, wt, ucol, rq, rk, kv0, kv1, rq3, rq2,
+           pos, direction, q, k, v, res, wbuf, urow, ldir, rq, rk, kv0, kv1, rq3, rq2,
            o_a, o_b2, o_b1, l_a, l_b2, l_b1, s_a, s_b2, s_c, t_a, t_b2, t_c,
-           st_acc, st_ml, att, keep, a_send, a_recv, b_send, b_recv, al_send, al_recv,
+           st_acc, st_ml, att, keep, turn, last, a_send, a_recv, b_send, b_recv, al_send, al_recv,
            lsem, ssem, rsem, xs, xr, als, alr):
     s = lax.axis_index("seq")
     t = lax.axis_index("tensor")
@@ -164,6 +164,8 @@
     x_peer = (t + 2) % 4
     half = wbuf.shape[2]
     width = half // 2
+    shift = (width // 128) * 128
+    window = half - shift
 
     local = {}
 
@@ -288,12 +290,12 @@
 
     def put(g, state, chunks):
         acc, _, l = state
-        out = (acc / l).astype(BF)
+        out = acc / l
         for i, c in enumerate(chunks):
             for h in (0, 1):
                 at = 256 * i + 128 * h
-                row = 256 * (2 * g + h)
-                att[c, row:row + 256, :] = out[:, at:at + 128]
+                col = 256 * (2 * g + h)
+                att[c, :, col:col + 256] = out[:, at:at + 128].T.astype(BF)
 
     def send_state(state, out_to, lse_to, *names):
         acc, m, l = state
@@ -311,17 +313,20 @@
         lanes = slice(256 * c, 256 * c + 256)
         return st_acc[g, :, lanes], st_ml[g, 0:1, lanes], st_ml[g, 8:9, lanes]
 
-    def prepare_weight():
+    def prepare_direction():
         local["dir"].wait()
         whole = direction[...].reshape(1, 2 * half)
         scale = 1.0 / jnp.sqrt(jnp.sum(whole * whole, axis=1, keepdims=True) + 1e-06)
+        lane = lax.broadcasted_iota(jnp.int32, (1, window), 1)
+        shared = jnp.where(core == 0, 0, shift)
+        keep_lane = (lane < shared) | (lane >= shared + (window - shift))
         for i, x in enumerate((x_other, x_here)):
-            local[i].wait()
             mine = jnp.where(x == 0, whole[:, :half], whole[:, half:]) * scale
-            for j in range(half // 128):
-                at = slice(128 * j, 128 * j + 128)
-                wt[i, at, :] = wbuf[i, :, at].T
-                ucol[i, at, :] = jnp.broadcast_to(mine[:, at], (128, 128)).T
+            low, high = mine[:, :window], mine[:, shift:]
+            urow[2 * i:2 * i + 1] = jnp.where(keep_lane, jnp.where(core == 0, high, low), 0.0)
+            urow[2 * i + 1:2 * i + 2] = jnp.where(core == 0, low, high)
+        for at in range(0, window, 128):
+            ldir[at:at + 128, :] = jnp.broadcast_to(urow[3:4, at:at + 128], (128, 128)).T
 
     @pl.when(s == 0)
     def _():
@@ -350,9 +355,7 @@
         start("q3a2")
         hold(1, attend(rq[1], [own(1)], True))
 
-    @pl.when(s != 1)
-    def _():
-        prepare_weight()
+    prepare_direction()
 
     @pl.when(s == 1)
     def _():
@@ -367,7 +370,6 @@
             state = attend(rq3[1, rows, :], [first(1), own(1)], False)
             send_state(state, s_c.at[1, c], t_c.at[1, c], "o3c" + n, "l3c" + n)
         put(1, attend(rq[1], [first(1), own(1)], True), (0, 1))
-        prepare_weight()
         recv("v0a1", "k0a1")
         put(0, attend(rq[0], [first(0), own(0)], True), (0, 1))
 
@@ -393,9 +395,12 @@
             device_id={"tensor": dev}, device_id_type=MESH)
 
     local["res"].wait()
-    own_part = pl.ds(pl.multiple_of(core * width, 64), width)
-    peer_part = pl.ds(pl.multiple_of((1 - core) * width, 64), width)
-    local_dir = ucol[1, own_part, :]
+    own_window = pl.ds(pl.multiple_of(core * shift, 128), window)
+    peer_window = pl.ds(pl.multiple_of((1 - core) * shift, 128), window)
+    own_rows = pl.ds(pl.multiple_of(core * (width - shift), 64), width)
+    local_dir = ldir[own_rows, :]
+    local[0].wait()
+    local[1].wait()
     a_copies, b_copies, al_copies = {}, {}, {}
     for c in (0, 1):
         lanes = slice(128 * c, 128 * c + 128)
@@ -410,22 +415,24 @@
             recv("o2b" + str(c), "l2b" + str(c))
             put(1, merge(held(1, c), o_b1[c], l_b1[c, 0:1]), (c,))
 
-        dots = jnp.sum(res[:, lanes].astype(F32) * local_dir, axis=0, keepdims=True)
+        dots = 0.0
         for i in (0, 1):
-            part = jnp.dot(wt[i, peer_part, :], att[c], preferred_element_type=F32)
+            part = jnp.dot(att[c], wbuf[i, :, peer_window], preferred_element_type=F32)
             a_send[c, i] = part.astype(BF)
             a_copies[c, i] = x_copy(a_send.at[c, i], a_recv.at[c, i], 2 * c + i, core_peer)
             a_copies[c, i].start()
-            dots = dots + jnp.sum(part * ucol[i, peer_part, :], axis=0, keepdims=True)
-            part = jnp.dot(wt[i, own_part, :], att[c], preferred_element_type=F32)
+            dots = dots + jnp.sum(part * urow[2 * i:2 * i + 1], axis=1, keepdims=True)
+            part = jnp.dot(att[c], wbuf[i, :, own_window], preferred_element_type=F32)
+            dots = dots + jnp.sum(part * urow[2 * i + 1:2 * i + 2], axis=1, keepdims=True)
+            keep[c, i] = part
             if i == 0:
                 a_copies[c, 0].wait_recv()
-                b_send[c] = (part + a_recv[c, 0].astype(F32)).astype(BF)
+                turn[...] = (keep[c, 0] + a_recv[c, 0].astype(F32)).T
+                b_send[c] = turn[own_rows, :].astype(BF)
                 b_copies[c] = x_copy(b_send.at[c], b_recv.at[c], 4 + c, x_peer)
                 b_copies[c].start()
-            else:
-                keep[c] = part
-            dots = dots + jnp.sum(part * ucol[i, own_part, :], axis=0, keepdims=True)
+        dots = jnp.broadcast_to(dots, (128, 128)).T[0:1]
+        dots = dots + jnp.sum(res[:, lanes].astype(F32) * local_dir, axis=0, keepdims=True)
         al_send[c] = jnp.broadcast_to(dots, (8, 128))
         for j in (1, 2, 3):
             i = 3 * c + j - 1
@@ -442,10 +449,11 @@
             al_copies[c, j].wait_recv()
             along = along + al_recv[c, j - 1]
         a_copies[c, 1].wait_recv()
-        hidden = res[:, lanes].astype(F32) + keep[c] + a_recv[c, 1].astype(F32)
-        keep[c] = hidden - along[0:1] * local_dir
+        turn[...] = (keep[c, 1] + a_recv[c, 1].astype(F32)).T
+        hidden = res[:, lanes].astype(F32) + turn[own_rows, :]
+        last[c] = hidden - along[0:1] * local_dir
         b_copies[c].wait_recv()
-        out_ref[:, lanes] = (keep[c] + b_recv[c].astype(F32)).astype(BF)
+        out_ref[:, lanes] = (last[c] + b_recv[c].astype(F32)).astype(BF)
 
     for c in (0, 1):
         a_copies[c, 0].wait_send()
@@ -475,6 +483,7 @@
     freqs = jnp.power(10000.0, -jnp.arange(HD // 2, dtype=F32) * 2.0 / HD)[None, :]
     rows, width = residual.shape
     depth = out_weight.shape[0]
+    window = 2 * width - (width // 128) * 128
     vmem = pl.BlockSpec(memory_space=pltpu.VMEM)
     anywhere = pl.BlockSpec(memory_space=pl.ANY)
     dma = pltpu.SemaphoreType.DMA
@@ -491,8 +500,8 @@
             pltpu.VMEM(value_rows.shape, BF),
             pltpu.VMEM((width, rows), BF),
             pltpu.VMEM((2, depth, 2 * width), BF),
-            pltpu.VMEM((2, 2 * width, depth), BF),
-            pltpu.VMEM((2, 2 * width, 128), F32),
+            pltpu.VMEM((8, window), F32),
+            pltpu.VMEM((window, 128), F32),
             pltpu.VMEM((2, 512, 256), BF),
             pltpu.VMEM((2, 256, 256), BF),
             pltpu.VMEM((4, 256, 256), BF),
@@ -513,10 +522,12 @@
             pltpu.VMEM((2, 2, 8, 256), F32),
             pltpu.VMEM((2, 256, 512), F32),
             pltpu.VMEM((2, 16, 512), F32),
-            pltpu.VMEM((2, depth, 128), BF),
+            pltpu.VMEM((2, 128, depth), BF),
+            pltpu.VMEM((2, 2, 128, window), F32),
+            pltpu.VMEM((window, 128), F32),
             pltpu.VMEM((2, width, 128), F32),
-            pltpu.VMEM((2, 2, width, 128), BF),
-            pltpu.VMEM((2, 2, width, 128), BF),
+            pltpu.VMEM((2, 2, 128, window), BF),
+            pltpu.VMEM((2, 2, 128, window), BF),
             pltpu.VMEM((2, width, 128), BF),
             pltpu.VMEM((2, width, 128), BF),
             pltpu.VMEM((2, 8, 128), F32),
@@ -544,7 +555,7 @@
         and queries.shape == (256, 1024)
         and key_rows.shape == (256, 512)
         and residual.shape[1] * 4 == direction.shape[0]
-        and residual.shape[1] % 64 == 0
+        and residual.shape[1] % 128 == 64
         and WINDOW == 1024
     )
     return fused_body(*args) if fits else body(*args)

time: 46.6 us -> 46.1 us (0.989)
  Pallas kernels: 44.1 us -> 43.6 us
where the time goes in v4:
time: 46.1 us; the launch traced here: 46 us
  Pallas kernels  43.6 us (95%)
  local copies, waits for them, and re-layouts  1.84 us (4%)
  other arithmetic  0.52 us (1%)
    pallas_call x1, Pallas kernels, fused_body(): pl.pallas_call(kernel, out_shape=jax.ShapeDtypeStruct((width, rows), BF),...  43.6 us
    unnamed x1, local copies, waits for them, and re-layouts  1.84 us

profile of v4, /device:TPU:25, one launch (start us, length us, event | category | flops | bytes accessed | tf_op | source)
XLA Modules:
  0.0 46.0 jit_solution(5762835650419280883)
XLA Ops:
  0.0 0.5 %multiply_power_fusion.freq_ref = f32[1,128]{1,0:T(1,128)} fusion(), kind=kLoop, calls=%fused_computation | loop fusion | flops 256 | bytes 512 | tf_op jit(solution)/shard_map/pow | solution.py:483
  0.5 43.6 %shard_map.73 = bf16[960,256]{1,0:T(8,128)(2,1)} custom-call(s32[256]{0:T(256)} %pos_hbm.1, f32[1,128]{1,0:T(1,128)} %multiply_power_fusion.freq_ref, bf16[256,1024]{1,0:T(8,128)(2,1)} %q_hbm.1, bf16[256,512]{1,0:T(8,128)(2,1)} %k_hbm.1, bf16[256,512]{1,0:T(8,128)(2,1)} %v_hbm.1, bf16[960,256]{1,0:T(8,128)(2,1)} %bitcast.3, f32[3840]{0:T(1024)} %dir_hbm.1, ...), custom_call_target="tpu_custom_call" | custom-call | tf_op jit(solution)/shard_map/pallas_call | solution.py:490
  44.1 1.8 %copy.9 = bf16[256,960]{0,1:T(8,128)(2,1)} copy(bf16[256,960]{0,1:T(8,128)(2,1)} %bitcast.2) | data formatting | bytes 983040

commit v5 on v4

--- a/solution.py
+++ b/solution.py
@@ -119,6 +119,21 @@
     x = x.astype(F32)
     a, b = x[:, :128], x[:, 128:]
     return jnp.concatenate([a * cos - b * sin, b * cos + a * sin], axis=1)
+
+
+def cos_sin(x):
+    n = jnp.floor(x * 0.15915494309189535 + 0.5)
+    r = ((x - n * 6.28125) - n * (507.0 / 262144.0)) - n * 1.2556659146019e-06
+    k = jnp.floor(r * 0.6366197723675814 + 0.5)
+    y = (r - k * 1.5707963705062866) + k * 4.371139000186241e-08
+    z = y * y
+    sin = y + y * z * (-1.0 / 6 + z * (1.0 / 120 + z * (-1.0 / 5040 + z * (1.0 / 362880))))
+    cos = 1.0 + z * (-0.5 + z * (1.0 / 24 + z * (-1.0 / 720 + z * (1.0 / 40320))))
+    odd = jnp.abs(k) == 1.0
+    flip = jnp.abs(k) == 2.0
+    cos_out = jnp.where(odd, -k * sin, jnp.where(flip, -cos, cos))
+    sin_out = jnp.where(odd, k * cos, jnp.where(flip, -sin, sin))
+    return cos_out, sin_out
 
 
 def attend(q, blocks, diag):
@@ -153,7 +168,8 @@
 def kernel(pos_hbm, freq_ref, q_hbm, k_hbm, v_hbm, res_hbm, dir_hbm, w_hbm, out_ref,
            pos, direction, q, k, v, res, wbuf, urow, ldir, rq, rk, kv0, kv1, rq3, rq2,
            o_a, o_b2, o_b1, l_a, l_b2, l_b1, s_a, s_b2, s_c, t_a, t_b2, t_c,
-           st_acc, st_ml, att, keep, turn, last, a_send, a_recv, b_send, b_recv, al_send, al_recv,
+           st_acc, st_ml, att, keep, dots, turn, last, a_send, a_recv, b_send, b_recv,
+           c_send, c_recv, al_send, al_recv,
            lsem, ssem, rsem, xs, xr, als, alr):
     s = lax.axis_index("seq")
     t = lax.axis_index("tensor")
@@ -206,13 +222,13 @@
     add("k0a2", 2, rk.at[0], kv0.at[0])
     add("v1a2", 2, v_hbm.at[:, 0:256], kv1.at[1])
     add("k1a2", 2, rk.at[0], kv1.at[0])
-    add("q3a2", 2, rq.at[0], rq3.at[0])
-    add("o3b", 3, s_b2, o_b2)
-    add("l3b", 3, t_b2, l_b2)
     for c in (0, 1):
         rows = slice(256 * c, 256 * c + 256)
         n = str(c)
         add("q3b2" + n, 2, rq.at[1, rows], rq3.at[1, rows])
+        add("q3a2" + n, 2, rq.at[0, rows], rq3.at[0, rows])
+        add("o3b" + n, 3, s_b2.at[c], o_b2.at[c])
+        add("l3b" + n, 3, t_b2.at[c], l_b2.at[c])
         add("f3b1" + n, 1, rq3.at[1, rows], rq3.at[1, rows])
         add("q2b1" + n, 1, rq.at[1, rows], rq2.at[rows])
         add("o3a" + n, 3, s_a.at[c], o_a.at[c])
@@ -236,7 +252,7 @@
 
     @pl.when(s == 0)
     def _():
-        start("v0b1", "v0a2")
+        start("v0b1")
 
     @pl.when(s == 1)
     def _():
@@ -248,17 +264,20 @@
     angles = jnp.concatenate(
         [jnp.broadcast_to(tokens[:, 128 * c:128 * c + 128], (128, 128)).T for c in (0, 1)], axis=0
     ) * freqs
-    cos, sin = jnp.cos(angles), jnp.sin(angles)
-    local["k"].wait()
-    for g in (1, 0):
-        rk[g] = rot(k[:, 256 * g:256 * g + 256], cos, sin).astype(BF)
+    cos, sin = cos_sin(angles)
+    def rotate_keys():
+        local["k"].wait()
+        for g in (1, 0):
+            rk[g] = rot(k[:, 256 * g:256 * g + 256], cos, sin).astype(BF)
 
     @pl.when(s == 0)
     def _():
-        start("k0b1", "k0a2")
+        rotate_keys()
+        start("k0b1")
 
     @pl.when(s == 1)
     def _():
+        rotate_keys()
         start("k1a2")
 
     local["q"].wait()
@@ -277,6 +296,10 @@
             def _():
                 start("q2b10")
 
+    @pl.when(s >= 2)
+    def _():
+        rotate_keys()
+
     local["v"].wait()
 
     def own(g):
@@ -295,7 +318,7 @@
             for h in (0, 1):
                 at = 256 * i + 128 * h
                 col = 256 * (2 * g + h)
-                att[c, :, col:col + 256] = out[:, at:at + 128].T.astype(BF)
+                att[128 * c:128 * c + 128, col:col + 256] = out[:, at:at + 128].T.astype(BF)
 
     def send_state(state, out_to, lse_to, *names):
         acc, m, l = state
@@ -330,9 +353,11 @@
 
     @pl.when(s == 0)
     def _():
+        sent("v0b1")
+        start("v0a2")
         put(1, attend(rq[1], [own(1)], True), (0, 1))
-        sent("v0b1", "v0a2")
-        start("v0a1", "k0a1")
+        sent("k0b1")
+        start("k0a2")
         put(0, attend(rq[0], [own(0)], True), (0, 1))
 
     @pl.when(s == 2)
@@ -341,21 +366,25 @@
         start("f3b10")
         sent("q2b10")
         start("q2b11")
+        state = attend(rq3[1, 0:256, :], [own(1)], False)
+        send_state(state, s_b2.at[0], t_b2.at[0], "o3b0", "l3b0")
         hold(1, attend(rq[1], [own(1)], True))
-        recv("q3b21")
-        start("f3b11")
-        send_state(attend(rq3[1], [own(1)], False), s_b2, t_b2, "o3b", "l3b")
 
     @pl.when(s == 3)
     def _():
         sent("q3b20")
+        start("q3a20")
+        hold(0, attend(rq[0], [own(0)], True))
+        sent("q3a20")
         start("q3b21")
-        hold(0, attend(rq[0], [own(0)], True))
-        sent("q3b21")
-        start("q3a2")
         hold(1, attend(rq[1], [own(1)], True))
 
     prepare_direction()
+
+    @pl.when(s == 0)
+    def _():
+        sent("v0a2", "k0a2")
+        start("v0a1", "k0a1")
 
     @pl.when(s == 1)
     def _():
@@ -375,9 +404,14 @@
 
     @pl.when(s == 2)
     def _():
-        recv("v1a2", "k1a2", "q3a2", "v0a2", "k0a2")
+        recv("q3b21")
+        start("f3b11")
+        state = attend(rq3[1, 256:512, :], [own(1)], False)
+        send_state(state, s_b2.at[1], t_b2.at[1], "o3b1", "l3b1")
+        recv("v1a2", "k1a2", "v0a2", "k0a2")
         for c in (0, 1):
             n = str(c)
+            recv("q3a2" + n)
             rows = slice(256 * c, 256 * c + 256)
             state = attend(rq3[0, rows, :], [first(0), second(), own(0)], False)
             send_state(state, s_a.at[c], t_a.at[c], "o3a" + n, "l3a" + n)
@@ -385,9 +419,8 @@
 
     @pl.when(s == 3)
     def _():
-        recv("o3b", "l3b")
-        acc, m, l = st_acc[1], st_ml[1, 0:1], st_ml[1, 8:9]
-        hold(1, merge((acc, m, l), o_b2[...], l_b2[0:1]))
+        sent("q3b21")
+        start("q3a21")
 
     def x_copy(src, dst, i, dev):
         return pltpu.make_async_remote_copy(
@@ -403,68 +436,79 @@
     local[1].wait()
     a_copies, b_copies, al_copies = {}, {}, {}
     for c in (0, 1):
-        lanes = slice(128 * c, 128 * c + 128)
-
         @pl.when(s == 3)
         def _(c=c):
-            recv("o3a" + str(c), "l3a" + str(c))
+            n = str(c)
+            recv("o3b" + n, "l3b" + n, "o3a" + n, "l3a" + n)
             put(0, merge(held(0, c), o_a[c], l_a[c, 0:1]), (c,))
-
-        @pl.when(s >= 2)
+            state = merge(held(1, c), o_b2[c], l_b2[c, 0:1])
+            recv("o2b" + n, "l2b" + n)
+            put(1, merge(state, o_b1[c], l_b1[c, 0:1]), (c,))
+
+        @pl.when(s == 2)
         def _(c=c):
             recv("o2b" + str(c), "l2b" + str(c))
             put(1, merge(held(1, c), o_b1[c], l_b1[c, 0:1]), (c,))
 
-        dots = 0.0
-        for i in (0, 1):
-            part = jnp.dot(att[c], wbuf[i, :, peer_window], preferred_element_type=F32)
-            a_send[c, i] = part.astype(BF)
-            a_copies[c, i] = x_copy(a_send.at[c, i], a_recv.at[c, i], 2 * c + i, core_peer)
-            a_copies[c, i].start()
-            dots = dots + jnp.sum(part * urow[2 * i:2 * i + 1], axis=1, keepdims=True)
-            part = jnp.dot(att[c], wbuf[i, :, own_window], preferred_element_type=F32)
-            dots = dots + jnp.sum(part * urow[2 * i + 1:2 * i + 2], axis=1, keepdims=True)
-            keep[c, i] = part
-            if i == 0:
-                a_copies[c, 0].wait_recv()
-                turn[...] = (keep[c, 0] + a_recv[c, 0].astype(F32)).T
-                b_send[c] = turn[own_rows, :].astype(BF)
-                b_copies[c] = x_copy(b_send.at[c], b_recv.at[c], 4 + c, x_peer)
-                b_copies[c].start()
-        dots = jnp.broadcast_to(dots, (128, 128)).T[0:1]
-        dots = dots + jnp.sum(res[:, lanes].astype(F32) * local_dir, axis=0, keepdims=True)
-        al_send[c] = jnp.broadcast_to(dots, (8, 128))
-        for j in (1, 2, 3):
-            i = 3 * c + j - 1
-            al_copies[c, j] = pltpu.make_async_remote_copy(
-                src_ref=al_send.at[c], dst_ref=al_recv.at[c, j - 1],
-                send_sem=als.at[i], recv_sem=alr.at[i],
-                device_id={"tensor": (t + j) % 4}, device_id_type=MESH)
-            al_copies[c, j].start()
-
+        rows = slice(128 * c, 128 * c + 128)
+        part = jnp.dot(att[rows, :], wbuf[0, :, peer_window], preferred_element_type=F32)
+        a_send[c] = part.astype(BF)
+        a_copies[c] = x_copy(a_send.at[c], a_recv.at[c], c, core_peer)
+        a_copies[c].start()
+        dots[rows, :] = part * urow[0:1]
+        part = jnp.dot(att[rows, :], wbuf[0, :, own_window], preferred_element_type=F32)
+        dots[rows, :] += part * urow[1:2]
+        keep[rows, :] = part
+        a_copies[c].wait_recv()
+        turn[...] = (keep[rows, :] + a_recv[c].astype(F32)).T
+        b_send[c] = turn[own_rows, :].astype(BF)
+        b_copies[c] = x_copy(b_send.at[c], b_recv.at[c], 4 + c, x_peer)
+        b_copies[c].start()
+
+    part = jnp.dot(att[...], wbuf[1, :, peer_window], preferred_element_type=F32)
+    c_send[...] = part.astype(BF)
+    c_copy = x_copy(c_send, c_recv, 2, core_peer)
+    c_copy.start()
+    dots[...] += part * urow[2:3]
+    part = jnp.dot(att[...], wbuf[1, :, own_window], preferred_element_type=F32)
+    keep[...] = part
+    total = jnp.sum(dots[...] + part * urow[3:4], axis=1, keepdims=True)
     for c in (0, 1):
         lanes = slice(128 * c, 128 * c + 128)
-        along = al_send[c]
-        for j in (1, 2, 3):
-            al_copies[c, j].wait_recv()
-            along = along + al_recv[c, j - 1]
-        a_copies[c, 1].wait_recv()
-        turn[...] = (keep[c, 1] + a_recv[c, 1].astype(F32)).T
-        hidden = res[:, lanes].astype(F32) + turn[own_rows, :]
-        last[c] = hidden - along[0:1] * local_dir
+        line = jnp.broadcast_to(total[lanes], (128, 128)).T[0:1]
+        line = line + jnp.sum(res[:, lanes].astype(F32) * local_dir, axis=0, keepdims=True)
+        al_send[:, lanes] = jnp.broadcast_to(line, (8, 128))
+    for j in (1, 2, 3):
+        al_copies[j] = pltpu.make_async_remote_copy(
+            src_ref=al_send, dst_ref=al_recv.at[j - 1],
+            send_sem=als.at[j - 1], recv_sem=alr.at[j - 1],
+            device_id={"tensor": (t + j) % 4}, device_id_type=MESH)
+        al_copies[j].start()
+    c_copy.wait_recv()
+    for c in (0, 1):
+        lanes = slice(128 * c, 128 * c + 128)
+        turn[...] = (keep[lanes, :] + c_recv[lanes, :].astype(F32)).T
+        last[:, lanes] = res[:, lanes].astype(F32) + turn[own_rows, :]
+    along = al_send[0:1]
+    for j in (1, 2, 3):
+        al_copies[j].wait_recv()
+        along = along + al_recv[j - 1, 0:1]
+    for c in (0, 1):
+        lanes = slice(128 * c, 128 * c + 128)
+        last[:, lanes] = last[:, lanes] - along[:, lanes] * local_dir
         b_copies[c].wait_recv()
-        out_ref[:, lanes] = (last[c] + b_recv[c].astype(F32)).astype(BF)
-
+        out_ref[:, lanes] = (last[:, lanes] + b_recv[c].astype(F32)).astype(BF)
+
+    c_copy.wait_send()
+    for j in (1, 2, 3):
+        al_copies[j].wait_send()
     for c in (0, 1):
-        a_copies[c, 0].wait_send()
-        a_copies[c, 1].wait_send()
+        a_copies[c].wait_send()
         b_copies[c].wait_send()
-        for j in (1, 2, 3):
-            al_copies[c, j].wait_send()
 
     @pl.when(s == 0)
     def _():
-        sent("k0b1", "k0a2", "v0a1", "k0a1")
+        sent("v0a1", "k0a1")
 
     @pl.when(s == 1)
     def _():
@@ -472,11 +516,11 @@
 
     @pl.when(s == 2)
     def _():
-        sent("q2b11", "f3b10", "f3b11", "o3b", "l3b", "o3a0", "l3a0", "o3a1", "l3a1")
+        sent("q2b11", "f3b10", "f3b11", "o3b0", "l3b0", "o3b1", "l3b1", "o3a0", "l3a0", "o3a1", "l3a1")
 
     @pl.when(s == 3)
     def _():
-        sent("q3a2")
+        sent("q3a21")
 
 
 def fused_body(queries, key_rows, value_rows, positions, residual, direction, out_weight):
@@ -509,32 +553,35 @@
             pltpu.VMEM((2, 512, 256), BF),
             pltpu.VMEM((512, 256), BF),
             pltpu.VMEM((2, 256, 256), BF),
-            pltpu.VMEM((256, 512), BF),
+            pltpu.VMEM((2, 256, 256), BF),
             pltpu.VMEM((2, 256, 256), BF),
             pltpu.VMEM((2, 8, 256), F32),
-            pltpu.VMEM((8, 512), F32),
+            pltpu.VMEM((2, 8, 256), F32),
             pltpu.VMEM((2, 8, 256), F32),
             pltpu.VMEM((2, 256, 256), BF),
-            pltpu.VMEM((256, 512), BF),
+            pltpu.VMEM((2, 256, 256), BF),
             pltpu.VMEM((2, 2, 256, 256), BF),
             pltpu.VMEM((2, 8, 256), F32),
-            pltpu.VMEM((8, 512), F32),
+            pltpu.VMEM((2, 8, 256), F32),
             pltpu.VMEM((2, 2, 8, 256), F32),
             pltpu.VMEM((2, 256, 512), F32),
             pltpu.VMEM((2, 16, 512), F32),
-            pltpu.VMEM((2, 128, depth), BF),
-            pltpu.VMEM((2, 2, 128, window), F32),
+            pltpu.VMEM((256, depth), BF),
+            pltpu.VMEM((256, window), F32),
+            pltpu.VMEM((256, window), F32),
             pltpu.VMEM((window, 128), F32),
-            pltpu.VMEM((2, width, 128), F32),
-            pltpu.VMEM((2, 2, 128, window), BF),
-            pltpu.VMEM((2, 2, 128, window), BF),
+            pltpu.VMEM((width, 256), F32),
+            pltpu.VMEM((2, 128, window), BF),
+            pltpu.VMEM((2, 128, window), BF),
             pltpu.VMEM((2, width, 128), BF),
             pltpu.VMEM((2, width, 128), BF),
-            pltpu.VMEM((2, 8, 128), F32),
-            pltpu.VMEM((2, 3, 8, 128), F32),
+            pltpu.VMEM((256, window), BF),
+            pltpu.VMEM((256, window), BF),
+            pltpu.VMEM((8, 256), F32),
+            pltpu.VMEM((3, 8, 256), F32),
             dma((8,)),
-            dma((29,)),
-            dma((29,)),
+            dma((32,)),
+            dma((32,)),
             dma((6,)),
             dma((6,)),
             dma((6,)),

time: 46.1 us -> 48.4 us (1.050)
  Pallas kernels: 43.6 us -> 45.8 us
    pallas_call x1, Pallas kernels: 43.6 us -> 45.8 us  [fused_body(): pl.pallas_call(kernel, out_shape=jax.ShapeDtypeStruct((width, rows), BF),...]
where the time goes in v5:
time: 48.4 us; the launch traced here: 48.2 us
  Pallas kernels  45.8 us (95%)
  local copies, waits for them, and re-layouts  1.84 us (4%)
  other arithmetic  0.52 us (1%)
    pallas_call x1, Pallas kernels, fused_body(): pl.pallas_call(kernel, out_shape=jax.ShapeDtypeStruct((width, rows), BF),...  45.8 us
    unnamed x1, local copies, waits for them, and re-layouts  1.84 us

profile of v5, /device:TPU:25, one launch (start us, length us, event | category | flops | bytes accessed | tf_op | source)
XLA Modules:
  0.0 48.2 jit_solution(1570473923648352487)
XLA Ops:
  0.0 0.5 %multiply_power_fusion.freq_ref = f32[1,128]{1,0:T(1,128)} fusion(), kind=kLoop, calls=%fused_computation | loop fusion | flops 256 | bytes 512 | tf_op jit(solution)/shard_map/pow | solution.py:527
  0.5 45.8 %shard_map.73 = bf16[960,256]{1,0:T(8,128)(2,1)} custom-call(s32[256]{0:T(256)} %pos_hbm.1, f32[1,128]{1,0:T(1,128)} %multiply_power_fusion.freq_ref, bf16[256,1024]{1,0:T(8,128)(2,1)} %q_hbm.1, bf16[256,512]{1,0:T(8,128)(2,1)} %k_hbm.1, bf16[256,512]{1,0:T(8,128)(2,1)} %v_hbm.1, bf16[960,256]{1,0:T(8,128)(2,1)} %bitcast.3, f32[3840]{0:T(1024)} %dir_hbm.1, ...), custom_call_target="tpu_custom_call" | custom-call | tf_op jit(solution)/shard_map/pallas_call | solution.py:534
  46.4 1.8 %copy.9 = bf16[256,960]{0,1:T(8,128)(2,1)} copy(bf16[256,960]{0,1:T(8,128)(2,1)} %bitcast.2) | data formatting | bytes 983040

commit v6 on v5

--- a/solution.py
+++ b/solution.py
@@ -252,7 +252,7 @@
 
     @pl.when(s == 0)
     def _():
-        start("v0b1")
+        start("v0b1", "v0a2")
 
     @pl.when(s == 1)
     def _():
@@ -273,7 +273,7 @@
     @pl.when(s == 0)
     def _():
         rotate_keys()
-        start("k0b1")
+        start("k0b1", "k0a2", "v0a1", "k0a1")
 
     @pl.when(s == 1)
     def _():
@@ -294,7 +294,7 @@
 
             @pl.when(s == 2)
             def _():
-                start("q2b10")
+                start("q2b10", "q2b11")
 
     @pl.when(s >= 2)
     def _():
@@ -353,38 +353,24 @@
 
     @pl.when(s == 0)
     def _():
-        sent("v0b1")
-        start("v0a2")
         put(1, attend(rq[1], [own(1)], True), (0, 1))
-        sent("k0b1")
-        start("k0a2")
         put(0, attend(rq[0], [own(0)], True), (0, 1))
 
     @pl.when(s == 2)
     def _():
         recv("q3b20")
         start("f3b10")
-        sent("q2b10")
-        start("q2b11")
         state = attend(rq3[1, 0:256, :], [own(1)], False)
         send_state(state, s_b2.at[0], t_b2.at[0], "o3b0", "l3b0")
         hold(1, attend(rq[1], [own(1)], True))
 
     @pl.when(s == 3)
     def _():
-        sent("q3b20")
-        start("q3a20")
+        start("q3a20", "q3b21", "q3a21")
         hold(0, attend(rq[0], [own(0)], True))
-        sent("q3a20")
-        start("q3b21")
         hold(1, attend(rq[1], [own(1)], True))
 
     prepare_direction()
-
-    @pl.when(s == 0)
-    def _():
-        sent("v0a2", "k0a2")
-        start("v0a1", "k0a1")
 
     @pl.when(s == 1)
     def _():
@@ -417,15 +403,27 @@
             send_state(state, s_a.at[c], t_a.at[c], "o3a" + n, "l3a" + n)
         put(0, attend(rq[0], [first(0), second(), own(0)], True), (0, 1))
 
-    @pl.when(s == 3)
-    def _():
-        sent("q3b21")
-        start("q3a21")
-
-    def x_copy(src, dst, i, dev):
-        return pltpu.make_async_remote_copy(
-            src_ref=src, dst_ref=dst, send_sem=xs.at[i], recv_sem=xr.at[i],
-            device_id={"tensor": dev}, device_id_type=MESH)
+    def x_copies(src, dst, first, dev):
+        part = src.shape[0] // 4
+        return [
+            pltpu.make_async_remote_copy(
+                src_ref=src.at[part * j:part * j + part], dst_ref=dst.at[part * j:part * j + part],
+                send_sem=xs.at[first + j], recv_sem=xr.at[first + j],
+                device_id={"tensor": dev}, device_id_type=MESH)
+            for j in range(4)
+        ]
+
+    def begin(parts):
+        for part in parts:
+            part.start()
+
+    def arrive(parts):
+        for part in parts:
+            part.wait_recv()
+
+    def leave(parts):
+        for part in parts:
+            part.wait_send()
 
     local["res"].wait()
     own_window = pl.ds(pl.multiple_of(core * shift, 128), window)
@@ -453,22 +451,22 @@
         rows = slice(128 * c, 128 * c + 128)
         part = jnp.dot(att[rows, :], wbuf[0, :, peer_window], preferred_element_type=F32)
         a_send[c] = part.astype(BF)
-        a_copies[c] = x_copy(a_send.at[c], a_recv.at[c], c, core_peer)
-        a_copies[c].start()
+        a_copies[c] = x_copies(a_send.at[c], a_recv.at[c], 4 * c, core_peer)
+        begin(a_copies[c])
         dots[rows, :] = part * urow[0:1]
         part = jnp.dot(att[rows, :], wbuf[0, :, own_window], preferred_element_type=F32)
         dots[rows, :] += part * urow[1:2]
         keep[rows, :] = part
-        a_copies[c].wait_recv()
+        arrive(a_copies[c])
         turn[...] = (keep[rows, :] + a_recv[c].astype(F32)).T
         b_send[c] = turn[own_rows, :].astype(BF)
-        b_copies[c] = x_copy(b_send.at[c], b_recv.at[c], 4 + c, x_peer)
-        b_copies[c].start()
+        b_copies[c] = x_copies(b_send.at[c], b_recv.at[c], 8 + 4 * c, x_peer)
+        begin(b_copies[c])
 
     part = jnp.dot(att[...], wbuf[1, :, peer_window], preferred_element_type=F32)
     c_send[...] = part.astype(BF)
-    c_copy = x_copy(c_send, c_recv, 2, core_peer)
-    c_copy.start()
+    c_copy = x_copies(c_send, c_recv, 16, core_peer)
+    begin(c_copy)
     dots[...] += part * urow[2:3]
     part = jnp.dot(att[...], wbuf[1, :, own_window], preferred_element_type=F32)
     keep[...] = part
@@ -484,7 +482,7 @@
             send_sem=als.at[j - 1], recv_sem=alr.at[j - 1],
             device_id={"tensor": (t + j) % 4}, device_id_type=MESH)
         al_copies[j].start()
-    c_copy.wait_recv()
+    arrive(c_copy)
     for c in (0, 1):
         lanes = slice(128 * c, 128 * c + 128)
         turn[...] = (keep[lanes, :] + c_recv[lanes, :].astype(F32)).T
@@ -496,19 +494,19 @@
     for c in (0, 1):
         lanes = slice(128 * c, 128 * c + 128)
         last[:, lanes] = last[:, lanes] - along[:, lanes] * local_dir
-        b_copies[c].wait_recv()
+        arrive(b_copies[c])
         out_ref[:, lanes] = (last[:, lanes] + b_recv[c].astype(F32)).astype(BF)
 
-    c_copy.wait_send()
+    leave(c_copy)
     for j in (1, 2, 3):
         al_copies[j].wait_send()
     for c in (0, 1):
-        a_copies[c].wait_send()
-        b_copies[c].wait_send()
+        leave(a_copies[c])
+        leave(b_copies[c])
 
     @pl.when(s == 0)
     def _():
-        sent("v0a1", "k0a1")
+        sent("v0b1", "k0b1", "v0a2", "k0a2", "v0a1", "k0a1")
 
     @pl.when(s == 1)
     def _():
@@ -516,11 +514,11 @@
 
     @pl.when(s == 2)
     def _():
-        sent("q2b11", "f3b10", "f3b11", "o3b0", "l3b0", "o3b1", "l3b1", "o3a0", "l3a0", "o3a1", "l3a1")
+        sent("q2b10", "q2b11", "f3b10", "f3b11", "o3b0", "l3b0", "o3b1", "l3b1", "o3a0", "l3a0", "o3a1", "l3a1")
 
     @pl.when(s == 3)
     def _():
-        sent("q3a21")
+        sent("q3b20", "q3a20", "q3b21", "q3a21")
 
 
 def fused_body(queries, key_rows, value_rows, positions, residual, direction, out_weight):
@@ -582,10 +580,10 @@
             dma((8,)),
             dma((32,)),
             dma((32,)),
-            dma((6,)),
-            dma((6,)),
-            dma((6,)),
-            dma((6,)),
+            dma((20,)),
+            dma((20,)),
+            dma((3,)),
+            dma((3,)),
         ],
         compiler_params=pltpu.CompilerParams(
             collective_id=0, has_side_effects=True, vmem_limit_bytes=60 * 1024 * 1024

time: 48.4 us -> 46.2 us (0.955)
  Pallas kernels: 45.8 us -> 43.7 us
    pallas_call x1, Pallas kernels: 45.8 us -> 43.7 us  [fused_body(): pl.pallas_call(kernel, out_shape=jax.ShapeDtypeStruct((width, rows), BF),...]
where the time goes in v6:
time: 46.2 us; the launch traced here: 46 us
  Pallas kernels  43.7 us (95%)
  local copies, waits for them, and re-layouts  1.84 us (4%)
  other arithmetic  0.52 us (1%)
    pallas_call x1, Pallas kernels, fused_body(): pl.pallas_call(kernel, out_shape=jax.ShapeDtypeStruct((width, rows), BF),...  43.7 us
    unnamed x1, local copies, waits for them, and re-layouts  1.84 us

profile of v6, /device:TPU:25, one launch (start us, length us, event | category | flops | bytes accessed | tf_op | source)
XLA Modules:
  0.0 46.0 jit_solution(1949688928466812310)
XLA Ops:
  0.0 0.5 %multiply_power_fusion.freq_ref = f32[1,128]{1,0:T(1,128)} fusion(), kind=kLoop, calls=%fused_computation | loop fusion | flops 256 | bytes 512 | tf_op jit(solution)/shard_map/pow | solution.py:525
  0.5 43.7 %shard_map.73 = bf16[960,256]{1,0:T(8,128)(2,1)} custom-call(s32[256]{0:T(256)} %pos_hbm.1, f32[1,128]{1,0:T(1,128)} %multiply_power_fusion.freq_ref, bf16[256,1024]{1,0:T(8,128)(2,1)} %q_hbm.1, bf16[256,512]{1,0:T(8,128)(2,1)} %k_hbm.1, bf16[256,512]{1,0:T(8,128)(2,1)} %v_hbm.1, bf16[960,256]{1,0:T(8,128)(2,1)} %bitcast.3, f32[3840]{0:T(1024)} %dir_hbm.1, ...), custom_call_target="tpu_custom_call" | custom-call | tf_op jit(solution)/shard_map/pallas_call | solution.py:532
  44.2 1.8 %copy.9 = bf16[256,960]{0,1:T(8,128)(2,1)} copy(bf16[256,960]{0,1:T(8,128)(2,1)} %bitcast.2) | data formatting | bytes 983040

commit v7 on v6

--- a/solution.py
+++ b/solution.py
@@ -218,8 +218,8 @@
         cols = slice(256 * g, 256 * g + 256)
         add("v0" + name + "1", 1, v_hbm.at[:, cols], kv0.at[2 * g + 1])
         add("k0" + name + "1", 1, rk.at[g], kv0.at[2 * g])
-    add("v0a2", 2, v_hbm.at[:, 0:256], kv0.at[1])
-    add("k0a2", 2, rk.at[0], kv0.at[0])
+    add("v0a2", 2, kv0.at[1], kv0.at[1])
+    add("k0a2", 2, kv0.at[0], kv0.at[0])
     add("v1a2", 2, v_hbm.at[:, 0:256], kv1.at[1])
     add("k1a2", 2, rk.at[0], kv1.at[0])
     for c in (0, 1):
@@ -252,7 +252,7 @@
 
     @pl.when(s == 0)
     def _():
-        start("v0b1", "v0a2")
+        start("v0b1")
 
     @pl.when(s == 1)
     def _():
@@ -273,7 +273,7 @@
     @pl.when(s == 0)
     def _():
         rotate_keys()
-        start("k0b1", "k0a2", "v0a1", "k0a1")
+        start("k0b1", "v0a1", "k0a1")
 
     @pl.when(s == 1)
     def _():
@@ -378,14 +378,16 @@
         for c in (0, 1):
             n = str(c)
             rows = slice(256 * c, 256 * c + 256)
+            recv("f3b1" + n)
+            state = attend(rq3[1, rows, :], [first(1), own(1)], False)
+            send_state(state, s_c.at[1, c], t_c.at[1, c], "o3c" + n, "l3c" + n)
             recv("q2b1" + n)
             state = attend(rq2[rows, :], [first(1), own(1)], False)
             send_state(state, s_c.at[0, c], t_c.at[0, c], "o2b" + n, "l2b" + n)
-            recv("f3b1" + n)
-            state = attend(rq3[1, rows, :], [first(1), own(1)], False)
-            send_state(state, s_c.at[1, c], t_c.at[1, c], "o3c" + n, "l3c" + n)
+            if c == 0:
+                recv("v0a1", "k0a1")
+                start("v0a2", "k0a2")
         put(1, attend(rq[1], [first(1), own(1)], True), (0, 1))
-        recv("v0a1", "k0a1")
         put(0, attend(rq[0], [first(0), own(0)], True), (0, 1))
 
     @pl.when(s == 2)
@@ -453,24 +455,24 @@
         a_send[c] = part.astype(BF)
         a_copies[c] = x_copies(a_send.at[c], a_recv.at[c], 4 * c, core_peer)
         begin(a_copies[c])
-        dots[rows, :] = part * urow[0:1]
         part = jnp.dot(att[rows, :], wbuf[0, :, own_window], preferred_element_type=F32)
-        dots[rows, :] += part * urow[1:2]
         keep[rows, :] = part
         arrive(a_copies[c])
         turn[...] = (keep[rows, :] + a_recv[c].astype(F32)).T
         b_send[c] = turn[own_rows, :].astype(BF)
         b_copies[c] = x_copies(b_send.at[c], b_recv.at[c], 8 + 4 * c, x_peer)
         begin(b_copies[c])
+        dots[rows, :] = a_send[c].astype(F32) * urow[0:1] + keep[rows, :] * urow[1:2]
 
     part = jnp.dot(att[...], wbuf[1, :, peer_window], preferred_element_type=F32)
     c_send[...] = part.astype(BF)
     c_copy = x_copies(c_send, c_recv, 16, core_peer)
     begin(c_copy)
-    dots[...] += part * urow[2:3]
     part = jnp.dot(att[...], wbuf[1, :, own_window], preferred_element_type=F32)
     keep[...] = part
-    total = jnp.sum(dots[...] + part * urow[3:4], axis=1, keepdims=True)
+    total = jnp.sum(
+        dots[...] + c_send[...].astype(F32) * urow[2:3] + part * urow[3:4], axis=1, keepdims=True
+    )
     for c in (0, 1):
         lanes = slice(128 * c, 128 * c + 128)
         line = jnp.broadcast_to(total[lanes], (128, 128)).T[0:1]
@@ -506,11 +508,11 @@
 
     @pl.when(s == 0)
     def _():
-        sent("v0b1", "k0b1", "v0a2", "k0a2", "v0a1", "k0a1")
+        sent("v0b1", "k0b1", "v0a1", "k0a1")
 
     @pl.when(s == 1)
     def _():
-        sent("v1a2", "k1a2", "o2b0", "l2b0", "o2b1", "l2b1", "o3c0", "l3c0", "o3c1", "l3c1")
+        sent("v1a2", "k1a2", "v0a2", "k0a2", "o2b0", "l2b0", "o2b1", "l2b1", "o3c0", "l3c0", "o3c1", "l3c1")
 
     @pl.when(s == 2)
     def _():

time: 46.2 us -> 52.6 us (1.14)
  Pallas kernels: 43.7 us -> 50 us
    pallas_call x1, Pallas kernels: 43.7 us -> 50 us  [fused_body(): pl.pallas_call(kernel, out_shape=jax.ShapeDtypeStruct((width, rows), BF),...]
where the time goes in v7:
time: 52.6 us; the launch traced here: 52.3 us
  Pallas kernels  50 us (95%)
  local copies, waits for them, and re-layouts  1.84 us (3%)
    pallas_call x1, Pallas kernels, fused_body(): pl.pallas_call(kernel, out_shape=jax.ShapeDtypeStruct((width, rows), BF),...  50 us
    unnamed x1, local copies, waits for them, and re-layouts  1.84 us

profile of v7, /device:TPU:25, one launch (start us, length us, event | category | flops | bytes accessed | tf_op | source)
XLA Modules:
  0.0 52.3 jit_solution(6177565202442775204)
XLA Ops:
  0.0 0.5 %multiply_power_fusion.freq_ref = f32[1,128]{1,0:T(1,128)} fusion(), kind=kLoop, calls=%fused_computation | loop fusion | flops 256 | bytes 512 | tf_op jit(solution)/shard_map/pow | solution.py:527
  0.5 50.0 %shard_map.73 = bf16[960,256]{1,0:T(8,128)(2,1)} custom-call(s32[256]{0:T(256)} %pos_hbm.1, f32[1,128]{1,0:T(1,128)} %multiply_power_fusion.freq_ref, bf16[256,1024]{1,0:T(8,128)(2,1)} %q_hbm.1, bf16[256,512]{1,0:T(8,128)(2,1)} %k_hbm.1, bf16[256,512]{1,0:T(8,128)(2,1)} %v_hbm.1, bf16[960,256]{1,0:T(8,128)(2,1)} %bitcast.3, f32[3840]{0:T(1024)} %dir_hbm.1, ...), custom_call_target="tpu_custom_call" | custom-call | tf_op jit(solution)/shard_map/pallas_call | solution.py:534
  50.5 1.8 %copy.9 = bf16[256,960]{0,1:T(8,128)(2,1)} copy(bf16[256,960]{0,1:T(8,128)(2,1)} %bitcast.2) | data formatting | bytes 983040

commit v8 on v7

--- a/solution.py
+++ b/solution.py
@@ -218,8 +218,8 @@
         cols = slice(256 * g, 256 * g + 256)
         add("v0" + name + "1", 1, v_hbm.at[:, cols], kv0.at[2 * g + 1])
         add("k0" + name + "1", 1, rk.at[g], kv0.at[2 * g])
-    add("v0a2", 2, kv0.at[1], kv0.at[1])
-    add("k0a2", 2, kv0.at[0], kv0.at[0])
+    add("v0a2", 2, v_hbm.at[:, 0:256], kv0.at[1])
+    add("k0a2", 2, rk.at[0], kv0.at[0])
     add("v1a2", 2, v_hbm.at[:, 0:256], kv1.at[1])
     add("k1a2", 2, rk.at[0], kv1.at[0])
     for c in (0, 1):
@@ -252,7 +252,7 @@
 
     @pl.when(s == 0)
     def _():
-        start("v0b1")
+        start("v0b1", "v0a2")
 
     @pl.when(s == 1)
     def _():
@@ -273,7 +273,7 @@
     @pl.when(s == 0)
     def _():
         rotate_keys()
-        start("k0b1", "v0a1", "k0a1")
+        start("k0b1", "k0a2")
 
     @pl.when(s == 1)
     def _():
@@ -354,6 +354,7 @@
     @pl.when(s == 0)
     def _():
         put(1, attend(rq[1], [own(1)], True), (0, 1))
+        start("v0a1", "k0a1")
         put(0, attend(rq[0], [own(0)], True), (0, 1))
 
     @pl.when(s == 2)
@@ -384,10 +385,8 @@
             recv("q2b1" + n)
             state = attend(rq2[rows, :], [first(1), own(1)], False)
             send_state(state, s_c.at[0, c], t_c.at[0, c], "o2b" + n, "l2b" + n)
-            if c == 0:
-                recv("v0a1", "k0a1")
-                start("v0a2", "k0a2")
         put(1, attend(rq[1], [first(1), own(1)], True), (0, 1))
+        recv("v0a1", "k0a1")
         put(0, attend(rq[0], [first(0), own(0)], True), (0, 1))
 
     @pl.when(s == 2)
@@ -508,11 +507,11 @@
 
     @pl.when(s == 0)
     def _():
-        sent("v0b1", "k0b1", "v0a1", "k0a1")
+        sent("v0b1", "k0b1", "v0a2", "k0a2", "v0a1", "k0a1")
 
     @pl.when(s == 1)
     def _():
-        sent("v1a2", "k1a2", "v0a2", "k0a2", "o2b0", "l2b0", "o2b1", "l2b1", "o3c0", "l3c0", "o3c1", "l3c1")
+        sent("v1a2", "k1a2", "o2b0", "l2b0", "o2b1", "l2b1", "o3c0", "l3c0", "o3c1", "l3c1")
 
     @pl.when(s == 2)
     def _():

time: 52.6 us -> 47.1 us (0.90)
  Pallas kernels: 50 us -> 44.2 us
    pallas_call x1, Pallas kernels: 50 us -> 44.2 us  [fused_body(): pl.pallas_call(kernel, out_shape=jax.ShapeDtypeStruct((width, rows), BF),...]
where the time goes in v8:
time: 47.1 us; the launch traced here: 46.6 us
  Pallas kernels  44.2 us (94%)
  local copies, waits for them, and re-layouts  1.84 us (4%)
  other arithmetic  0.52 us (1%)
    pallas_call x1, Pallas kernels, fused_body(): pl.pallas_call(kernel, out_shape=jax.ShapeDtypeStruct((width, rows), BF),...  44.2 us
    unnamed x1, local copies, waits for them, and re-layouts  1.84 us

profile of v8, /device:TPU:25, one launch (start us, length us, event | category | flops | bytes accessed | tf_op | source)
XLA Modules:
  0.0 46.6 jit_solution(12642291039273675532)
XLA Ops:
  0.0 0.5 %multiply_power_fusion.freq_ref = f32[1,128]{1,0:T(1,128)} fusion(), kind=kLoop, calls=%fused_computation | loop fusion | flops 256 | bytes 512 | tf_op jit(solution)/shard_map/pow | solution.py:526
  0.5 44.2 %shard_map.73 = bf16[960,256]{1,0:T(8,128)(2,1)} custom-call(s32[256]{0:T(256)} %pos_hbm.1, f32[1,128]{1,0:T(1,128)} %multiply_power_fusion.freq_ref, bf16[256,1024]{1,0:T(8,128)(2,1)} %q_hbm.1, bf16[256,512]{1,0:T(8,128)(2,1)} %k_hbm.1, bf16[256,512]{1,0:T(8,128)(2,1)} %v_hbm.1, bf16[960,256]{1,0:T(8,128)(2,1)} %bitcast.3, f32[3840]{0:T(1024)} %dir_hbm.1, ...), custom_call_target="tpu_custom_call" | custom-call | tf_op jit(solution)/shard_map/pallas_call | solution.py:533
  44.7 1.8 %copy.9 = bf16[256,960]{0,1:T(8,128)(2,1)} copy(bf16[256,960]{0,1:T(8,128)(2,1)} %bitcast.2) | data formatting | bytes 983040

commit v9 on v8

--- a/solution.py
+++ b/solution.py
@@ -252,7 +252,7 @@
 
     @pl.when(s == 0)
     def _():
-        start("v0b1", "v0a2")
+        start("v0a2")
 
     @pl.when(s == 1)
     def _():
@@ -273,7 +273,7 @@
     @pl.when(s == 0)
     def _():
         rotate_keys()
-        start("k0b1", "k0a2")
+        start("k0a2")
 
     @pl.when(s == 1)
     def _():
@@ -353,6 +353,7 @@
 
     @pl.when(s == 0)
     def _():
+        start("v0b1", "k0b1")
         put(1, attend(rq[1], [own(1)], True), (0, 1))
         start("v0a1", "k0a1")
         put(0, attend(rq[0], [own(0)], True), (0, 1))
@@ -379,12 +380,12 @@
         for c in (0, 1):
             n = str(c)
             rows = slice(256 * c, 256 * c + 256)
+            recv("q2b1" + n)
+            state = attend(rq2[rows, :], [first(1), own(1)], False)
+            send_state(state, s_c.at[0, c], t_c.at[0, c], "o2b" + n, "l2b" + n)
             recv("f3b1" + n)
             state = attend(rq3[1, rows, :], [first(1), own(1)], False)
             send_state(state, s_c.at[1, c], t_c.at[1, c], "o3c" + n, "l3c" + n)
-            recv("q2b1" + n)
-            state = attend(rq2[rows, :], [first(1), own(1)], False)
-            send_state(state, s_c.at[0, c], t_c.at[0, c], "o2b" + n, "l2b" + n)
         put(1, attend(rq[1], [first(1), own(1)], True), (0, 1))
         recv("v0a1", "k0a1")
         put(0, attend(rq[0], [first(0), own(0)], True), (0, 1))

time: 47.1 us -> 46.4 us (0.985)
  no operation moved by 1% of the time
where the time goes in v9:
time: 46.4 us; the launch traced here: 46.2 us
  Pallas kernels  43.8 us (94%)
  local copies, waits for them, and re-layouts  1.84 us (4%)
  other arithmetic  0.52 us (1%)
    pallas_call x1, Pallas kernels, fused_body(): pl.pallas_call(kernel, out_shape=jax.ShapeDtypeStruct((width, rows), BF),...  43.8 us
    unnamed x1, local copies, waits for them, and re-layouts  1.84 us

profile of v9, /device:TPU:25, one launch (start us, length us, event | category | flops | bytes accessed | tf_op | source)
XLA Modules:
  0.0 46.2 jit_solution(535845895427655383)
XLA Ops:
  0.0 0.5 %multiply_power_fusion.freq_ref = f32[1,128]{1,0:T(1,128)} fusion(), kind=kLoop, calls=%fused_computation | loop fusion | flops 256 | bytes 512 | tf_op jit(solution)/shard_map/pow | solution.py:527
  0.5 43.8 %shard_map.73 = bf16[960,256]{1,0:T(8,128)(2,1)} custom-call(s32[256]{0:T(256)} %pos_hbm.1, f32[1,128]{1,0:T(1,128)} %multiply_power_fusion.freq_ref, bf16[256,1024]{1,0:T(8,128)(2,1)} %q_hbm.1, bf16[256,512]{1,0:T(8,128)(2,1)} %k_hbm.1, bf16[256,512]{1,0:T(8,128)(2,1)} %v_hbm.1, bf16[960,256]{1,0:T(8,128)(2,1)} %bitcast.3, f32[3840]{0:T(1024)} %dir_hbm.1, ...), custom_call_target="tpu_custom_call" | custom-call | tf_op jit(solution)/shard_map/pallas_call | solution.py:534
  44.4 1.8 %copy.9 = bf16[256,960]{0,1:T(8,128)(2,1)} copy(bf16[256,960]{0,1:T(8,128)(2,1)} %bitcast.2) | data formatting | bytes 983040
